TPU v7x, 32 devices: a whole 2x2x4 slice. The times are simulated.
32 devices in a mesh: dp: 16 (over z, y, x), head: 2 (over core).
Axes of the slice: x: 2, y: 2, z: 4, core: 2. Of those that a mesh axis runs over, the one named last changes fastest.
Arguments:
- master: float32 [2, 5412864], P('head', 'dp'), as said below
- first_moment: float32 [2, 5412864], P('head', 'dp'), as said below
- second_moment: float32 [2, 5412864], P('head', 'dp'), as said below
- token_ids: int32 [32, 512], P('dp'), may hold values from 0 to 30521
- token_types: int32 [32, 512], P('dp'), may hold values from 0 to 1
- counts: int32 [32, 8], P('dp'), may hold values from 1 to 256, 512 in all within a row
- mask_pos: int32 [32, 40], P('dp'), may hold values from 0 to 255
- teacher_states: bfloat16 [32, 512, 768], P('dp'), may hold values from -6 to 6
- teacher_qk: bfloat16 [768, 2, 768], P(None, None, 'head'), may hold values from -0.21875 to 0.21875
- mentor_logits: bfloat16 [32, 40, 30522], P('dp', None, 'head'), may hold values from -16 to 16
Outputs:
- loss_sum: float32 [], replicated
- grad_norm: float32 [], replicated
- new_master: float32 [2, 5412864], P('head', 'dp')
- new_first: float32 [2, 5412864], P('head', 'dp')
- new_second: float32 [2, 5412864], P('head', 'dp')
- new_weights: bfloat16 [2, 5412864], P('head', 'dp')
Inputs may be any that keep to these rules, and one draw needn't show every extreme that they name: `counts`: the last entry of a row is its padding; the others count its sentences' tokens; a row's entries sum to 512. `mask_pos`: masked positions lie before a row's padding and may repeat. `master`: entries from 5412864 on are zero. `first_moment`: entries from 5412864 on are zero. `second_moment`: every entry is positive.
All inputs are finite; a program needn't handle non-finite values.
Results may differ from a plain program's by a relative error of at most 0.0035.
The roundings to bfloat16 on the way count: a program that leaves them out, or rounds other values in their place, can miss the bound.
Values may be sent and summed in bfloat16 or wider, within the bound.
No kernel may reach another device: no remote copies, remote signals or barrier semaphores. Data moves between devices by JAX's collectives and lax.ppermute only.
A program may use at most 256 MiB of HBM per device.

v0:
```python
import math

import jax
import jax.numpy as jnp
from jax import lax
from jax.sharding import PartitionSpec as P

D = 312
HD = 26
FF = 1200
VOCAB = 30522
THD = 64
LAYERS = 1
LEN = 512
MICRO = 2
STEP = 10
SROWS = 522


ATT_WEIGHT = 1.0
SOFTEN_FACTOR = 2.0
CLIP_NORM = 1.0
BETA_ONE = 0.9
BETA_TWO = 0.999
RATE_MATRIX = 0.06
RATE_VECTOR = 0.6
WEIGHT_DECAY = 0.01
ADAM_EPS = 1e-08
NORM_EPS = 1e-12
MASKED = -1000000000.0


def gather_rows(value):
    return lax.all_gather(value, "head", axis=0, tiled=True)


def scatter_rows(value):
    return lax.psum_scatter(
        value.astype(jnp.bfloat16), "head", scatter_dimension=0, tiled=True
    ).astype(jnp.float32)


def gather_back(value):
    return lax.all_gather(value, "head", axis=0, tiled=True)


def scatter_back(value):
    return lax.psum_scatter(
        value.astype(jnp.bfloat16), "head", scatter_dimension=0, tiled=True
    ).astype(jnp.float32)


def unpack(flat_weights, head_total):
    width_head = D // head_total
    units_head = FF // head_total
    vocab_head = VOCAB // head_total
    shapes = [
        (vocab_head, D),
        (LAYERS, 3, D, width_head),
        (LAYERS, width_head, D),
        (LAYERS, D, units_head),
        (LAYERS, units_head, D),
        (SROWS, width_head),
        (LAYERS, 2, width_head),
        (LAYERS, units_head),
    ]
    result = []
    offset = 0
    for piece_shape in shapes:
        length = math.prod(piece_shape)
        result.append(flat_weights[offset : offset + length].reshape(piece_shape))
        offset += length
    return result


def structure(counts):
    sentence_ends = jnp.cumsum(counts, axis=-1)
    positions = jnp.arange(LEN, dtype=jnp.int32)
    passed = (positions[None, :, None] >= sentence_ends[:, None, :]).astype(jnp.int32)
    sentence = jnp.sum(passed, axis=-1)
    within = positions[None, :] - jnp.sum(passed * counts[:, None, :], axis=-1)
    return (sentence, within)


def norm_forward(value, gain_row, bias_row):
    centred = value - jnp.mean(value, axis=-1, keepdims=True)
    inverse = lax.rsqrt(jnp.mean(centred * centred, axis=-1, keepdims=True) + NORM_EPS)
    normed = centred * inverse
    return (normed * gain_row + bias_row, (normed, inverse))


def norm_backward(gradient, saved, gain_row):
    normed, inverse = saved
    scaled = gradient * gain_row
    inner_part = (
        scaled
        - jnp.mean(scaled, -1, keepdims=True)
        - normed * jnp.mean(scaled * normed, -1, keepdims=True)
    )
    return (inner_part * inverse, jnp.sum(gradient * normed, 0), jnp.sum(gradient, 0))


def attention_probs(queries, key_heads, allowed, score_scale, log_total):
    scores = (
        jnp.einsum("rheq,rhek->rhqk", queries, key_heads, preferred_element_type=jnp.float32)
        * score_scale
    )
    scores = jnp.where(allowed, scores, MASKED)
    if log_total is None:
        row_top = jnp.max(scores, axis=-1, keepdims=True)
        exponent = jnp.exp(scores - row_top)
        totals = jnp.sum(exponent, axis=-1, keepdims=True)
        return (exponent / totals, row_top + jnp.log(totals))
    return (jnp.exp(scores - log_total), log_total)


def layer_forward(hidden_state, layer_weights, shared_rows, context):
    attn_in, attn_out, ffn_in, ffn_out, qv_bias, up_bias = layer_weights
    allowed, valid_rows, teacher_prob = context
    row_count = allowed.shape[0]
    local_width = attn_out.shape[0]
    head_count = local_width // HD
    gathered = gather_rows(hidden_state.astype(jnp.bfloat16)).reshape(row_count, LEN, D)
    qkv_bias = jnp.stack([qv_bias[0], jnp.zeros_like(qv_bias[0]), qv_bias[1]])
    projected = (
        jnp.einsum("rld,cde->rcel", gathered, attn_in, preferred_element_type=jnp.float32)
        + qkv_bias[None, :, :, None]
    )
    projected = projected.astype(jnp.bfloat16)
    heads_view = projected.reshape(row_count, 3, head_count, HD, LEN)
    attn_prob, log_total = attention_probs(
        heads_view[:, 0], heads_view[:, 1], allowed, HD ** (-0.5), None
    )
    mismatch = attn_prob - teacher_prob
    map_loss = ATT_WEIGHT * jnp.sum(mismatch * mismatch * valid_rows)
    mixed_heads = jnp.einsum(
        "rhqk,rhek->rheq",
        attn_prob.astype(jnp.bfloat16),
        heads_view[:, 2],
        preferred_element_type=jnp.float32,
    )
    mixed_heads = mixed_heads.astype(jnp.bfloat16).reshape(row_count, local_width, LEN)
    attended = scatter_rows(
        jnp.einsum(
            "rel,ed->rld", mixed_heads, attn_out, preferred_element_type=jnp.float32
        ).reshape(-1, D)
    )
    state_one, saved_one = norm_forward(
        hidden_state + attended + shared_rows[4], shared_rows[0], shared_rows[1]
    )
    gathered_one = gather_rows(state_one.astype(jnp.bfloat16))
    pre_act = jnp.dot(gathered_one, ffn_in, preferred_element_type=jnp.float32) + up_bias
    hidden_act = jax.nn.gelu(pre_act, approximate=False).astype(jnp.bfloat16)
    branch = scatter_rows(jnp.dot(hidden_act, ffn_out, preferred_element_type=jnp.float32))
    state_two, saved_two = norm_forward(
        state_one + branch + shared_rows[5], shared_rows[2], shared_rows[3]
    )
    saved = (
        gathered,
        projected,
        log_total,
        mixed_heads,
        saved_one,
        gathered_one,
        pre_act,
        hidden_act,
        saved_two,
    )
    return (state_two, map_loss, saved)


def layer_backward(gradient, layer_weights, shared_rows, saved, context):
    attn_in, attn_out, ffn_in, ffn_out, qv_bias, up_bias = layer_weights
    allowed, valid_rows, teacher_prob = context
    (
        gathered,
        projected,
        log_total,
        mixed_heads,
        saved_one,
        gathered_one,
        pre_act,
        hidden_act,
        saved_two,
    ) = saved
    row_count = allowed.shape[0]
    local_width = attn_out.shape[0]
    head_count = local_width // HD
    score_scale = HD ** (-0.5)
    grad_res, gain_two, bias_two = norm_backward(gradient, saved_two, shared_rows[2])
    grad_branch = gather_back(grad_res.astype(jnp.bfloat16))
    grad_ffn_out = jnp.einsum(
        "tf,td->fd", hidden_act, grad_branch, preferred_element_type=jnp.float32
    )
    grad_hidden = jnp.einsum("td,fd->tf", grad_branch, ffn_out, preferred_element_type=jnp.float32)
    _, gelu_pull = jax.vjp(lambda value: jax.nn.gelu(value, approximate=False), pre_act)
    grad_pre = gelu_pull(grad_hidden)[0].astype(jnp.bfloat16)
    grad_ffn_in = jnp.einsum(
        "td,tf->df", gathered_one, grad_pre, preferred_element_type=jnp.float32
    )
    grad_up_bias = jnp.sum(grad_pre.astype(jnp.float32), 0)
    grad_one = grad_res + scatter_back(
        jnp.einsum("tf,df->td", grad_pre, ffn_in, preferred_element_type=jnp.float32)
    )
    grad_mid, gain_one, bias_one = norm_backward(grad_one, saved_one, shared_rows[0])
    grad_attended = gather_back(grad_mid.astype(jnp.bfloat16)).reshape(row_count, LEN, D)
    grad_attn_out = jnp.einsum(
        "rel,rld->ed", mixed_heads, grad_attended, preferred_element_type=jnp.float32
    )
    grad_mixed = jnp.einsum(
        "rld,ed->rel", grad_attended, attn_out, preferred_element_type=jnp.float32
    )
    grad_mixed = grad_mixed.astype(jnp.bfloat16).reshape(row_count, head_count, HD, LEN)
    heads_view = projected.reshape(row_count, 3, head_count, HD, LEN)
    queries, key_heads, values = (heads_view[:, 0], heads_view[:, 1], heads_view[:, 2])
    attn_prob, _ = attention_probs(queries, key_heads, allowed, score_scale, log_total)
    grad_prob = jnp.einsum(
        "rheq,rhek->rhqk", grad_mixed, values, preferred_element_type=jnp.float32
    )
    grad_prob = grad_prob + 2.0 * ATT_WEIGHT * (attn_prob - teacher_prob) * valid_rows
    grad_values = jnp.einsum(
        "rhqk,rheq->rhek",
        attn_prob.astype(jnp.bfloat16),
        grad_mixed,
        preferred_element_type=jnp.float32,
    )
    grad_scores = attn_prob * (grad_prob - jnp.sum(attn_prob * grad_prob, -1, keepdims=True))
    grad_scores = grad_scores.astype(jnp.bfloat16)
    grad_queries = (
        jnp.einsum("rhqk,rhek->rheq", grad_scores, key_heads, preferred_element_type=jnp.float32)
        * score_scale
    )
    grad_keys = (
        jnp.einsum("rhqk,rheq->rhek", grad_scores, queries, preferred_element_type=jnp.float32)
        * score_scale
    )
    grad_proj = (
        jnp.stack([grad_queries, grad_keys, grad_values], axis=1)
        .astype(jnp.bfloat16)
        .reshape(row_count, 3, local_width, LEN)
    )
    grad_attn_in = jnp.einsum(
        "rld,rcel->cde", gathered, grad_proj, preferred_element_type=jnp.float32
    )
    summed = jnp.sum(grad_proj.astype(jnp.float32), axis=(0, 3))
    grad_qv_bias = jnp.stack([summed[0], summed[2]])
    grad_in = grad_mid + scatter_back(
        jnp.einsum("rcel,cde->rld", grad_proj, attn_in, preferred_element_type=jnp.float32).reshape(
            -1, D
        )
    )
    grad_shared = jnp.stack(
        [gain_one, bias_one, gain_two, bias_two, jnp.sum(grad_mid, 0), jnp.sum(grad_res, 0)]
    )
    return (
        grad_in,
        (grad_attn_in, grad_attn_out, grad_ffn_in, grad_ffn_out, grad_qv_bias, grad_up_bias),
        grad_shared,
    )


def micro_step(
    pieces, weight_stacks, shared, word_embedding_matrix, teacher_qk, head_index, head_total
):
    token_ids, token_types, counts, mask_pos, teacher_in, mentor_logits = pieces
    row_count = token_ids.shape[0]
    token_count = row_count * LEN
    half_count = token_count // head_total
    first_row = head_index * half_count
    vocabulary_local_slice = word_embedding_matrix.shape[0]
    sentence, within = structure(counts)
    allowed = (sentence[:, :, None] == sentence[:, None, :])[:, None]
    valid_rows = (sentence < counts.shape[1] - 1).astype(jnp.float32)[:, None, :, None]
    teacher_proj = jnp.einsum(
        "rld,dce->rcel", teacher_in, teacher_qk, preferred_element_type=jnp.float32
    ).astype(jnp.bfloat16)
    teacher_heads = teacher_proj.shape[2] // THD
    teacher_view = teacher_proj.reshape(row_count, 2, teacher_heads, THD, LEN)
    teacher_prob, _ = attention_probs(
        teacher_view[:, 0], teacher_view[:, 1], allowed, THD ** (-0.5), None
    )
    context = (allowed, valid_rows, teacher_prob)
    local_ids = token_ids.reshape(-1) - head_index * vocabulary_local_slice
    inside = (local_ids >= 0) & (local_ids < vocabulary_local_slice)
    safe_ids = jnp.clip(local_ids, 0, vocabulary_local_slice - 1)
    word_part = jnp.where(inside[:, None], word_embedding_matrix[safe_ids].astype(jnp.float32), 0.0)
    words = lax.psum_scatter(
        word_part.astype(jnp.bfloat16), "head", scatter_dimension=0, tiled=True
    ).astype(jnp.float32)
    own_pos = lax.dynamic_slice_in_dim(within.reshape(-1), first_row, half_count)
    own_types = lax.dynamic_slice_in_dim(token_types.reshape(-1), first_row, half_count)
    hidden_state, embed_saved = norm_forward(
        words + shared[own_pos] + shared[LEN + own_types], shared[LEN + 2], shared[LEN + 3]
    )
    layer_index = 0
    row_base = LEN + 4 + 6 * layer_index
    layer_weights = tuple((stack_item[layer_index] for stack_item in weight_stacks))
    hidden_state, loss_term, saved = layer_forward(
        hidden_state, layer_weights, shared[row_base : row_base + 6], context
    )
    stored = [saved]
    final_rows = gather_rows(hidden_state.astype(jnp.bfloat16))
    picked = (jnp.arange(row_count, dtype=jnp.int32)[:, None] * LEN + mask_pos).reshape(-1)
    picked_logit = final_rows[picked]
    pupil_logits = (
        jnp.einsum(
            "md,vd->mv", picked_logit, word_embedding_matrix, preferred_element_type=jnp.float32
        )
        / SOFTEN_FACTOR
    )
    teacher_logits_scaled = (
        mentor_logits.reshape(-1, vocabulary_local_slice).astype(jnp.float32) / SOFTEN_FACTOR
    )
    student_top, teacher_top = lax.pmax(
        (jnp.max(pupil_logits, -1), jnp.max(teacher_logits_scaled, -1)), "head"
    )
    student_exponent_values = jnp.exp(pupil_logits - student_top[:, None])
    teacher_exponent_values = jnp.exp(teacher_logits_scaled - teacher_top[:, None])
    student_exponent_sum, teacher_exponent_sum, cross_sum = lax.psum(
        (
            jnp.sum(student_exponent_values, -1),
            jnp.sum(teacher_exponent_values, -1),
            jnp.sum(teacher_exponent_values * pupil_logits, -1),
        ),
        "head",
    )
    entropy = jnp.sum(
        student_top + jnp.log(student_exponent_sum) - cross_sum / teacher_exponent_sum
    )
    grad_logits = (
        (
            student_exponent_values / student_exponent_sum[:, None]
            - teacher_exponent_values / teacher_exponent_sum[:, None]
        )
        / SOFTEN_FACTOR
    ).astype(jnp.bfloat16)
    grad_table = jnp.einsum(
        "mv,md->vd", grad_logits, picked_logit, preferred_element_type=jnp.float32
    )
    grad_chosen = jnp.einsum(
        "mv,vd->md", grad_logits, word_embedding_matrix, preferred_element_type=jnp.float32
    )
    gradient = scatter_back(jnp.zeros((token_count, D), jnp.float32).at[picked].add(grad_chosen))
    layer_grads = [None] * LAYERS
    shared_grads = [None] * LAYERS
    for layer_index in reversed(range(LAYERS)):
        row_base = LEN + 4 + 6 * layer_index
        layer_weights = tuple((stack_item[layer_index] for stack_item in weight_stacks))
        gradient, layer_grads[layer_index], shared_grads[layer_index] = layer_backward(
            gradient, layer_weights, shared[row_base : row_base + 6], stored[layer_index], context
        )
    grad_embed, gain_embed, bias_embed = norm_backward(gradient, embed_saved, shared[LEN + 2])
    top_rows = (
        jnp.zeros((LEN + 2, D), jnp.float32)
        .at[own_pos]
        .add(grad_embed)
        .at[LEN + own_types]
        .add(grad_embed)
    )
    grad_shared = jnp.concatenate(
        [top_rows, gain_embed[None], bias_embed[None]] + shared_grads, axis=0
    )
    grad_words = gather_back(grad_embed.astype(jnp.bfloat16))
    grad_table = grad_table + jnp.zeros_like(grad_table).at[safe_ids].add(
        jnp.where(inside[:, None], grad_words.astype(jnp.float32), 0.0)
    )
    stacked = [
        jnp.stack([layer_grad[kind_index] for layer_grad in layer_grads]) for kind_index in range(6)
    ]
    grads = (
        grad_table,
        stacked[0],
        stacked[1],
        stacked[2],
        stacked[3],
        grad_shared,
        stacked[4],
        stacked[5],
    )
    return (grads, loss_term + entropy / head_total)


def reduce_grads(grads, flat_width):
    grad_table, grad_in, grad_out, grad_up, grad_down, grad_shared, grad_qv, grad_bias = grads
    shared_half = lax.psum_scatter(
        grad_shared.astype(jnp.bfloat16), "head", scatter_dimension=1, tiled=True
    ).astype(jnp.float32)
    members = [
        member.reshape(-1)
        for member in (
            grad_table,
            grad_in,
            grad_out,
            grad_up,
            grad_down,
            shared_half,
            grad_qv,
            grad_bias,
        )
    ]
    used_count = sum((member_flat.shape[0] for member_flat in members))
    joined = jnp.concatenate(members + [jnp.zeros((flat_width - used_count,), jnp.float32)])
    return lax.psum_scatter(joined[None], "dp", scatter_dimension=1, tiled=True)


def local(
    master,
    first_moment,
    second_moment,
    token_ids,
    token_types,
    counts,
    mask_pos,
    teacher_states,
    teacher_qk,
    mentor_logits,
):
    head_total = lax.axis_size("head")
    head_index = lax.axis_index("head")
    flat_weights = lax.all_gather(master.astype(jnp.bfloat16), "dp", axis=1, tiled=True)[0]
    flat_width = flat_weights.shape[0]
    word_embedding_matrix, attn_in, attn_out, ffn_in, ffn_out, shared_half, qv_bias, up_bias = (
        unpack(flat_weights, head_total)
    )
    shared = lax.all_gather(shared_half, "head", axis=1, tiled=True).astype(jnp.float32)
    weight_stacks = (
        attn_in,
        attn_out,
        ffn_in,
        ffn_out,
        qv_bias.astype(jnp.float32),
        up_bias.astype(jnp.float32),
    )
    micro_rows = token_ids.shape[0] // MICRO
    loss_local = jnp.zeros((), jnp.float32)
    summed = None
    for micro_index in range(MICRO):
        low_row = micro_index * micro_rows
        pieces = tuple(
            (
                source[low_row : low_row + micro_rows]
                for source in (
                    token_ids,
                    token_types,
                    counts,
                    mask_pos,
                    teacher_states,
                    mentor_logits,
                )
            )
        )
        grads, loss_term = micro_step(
            pieces, weight_stacks, shared, word_embedding_matrix, teacher_qk, head_index, head_total
        )
        loss_local = loss_local + loss_term
        summed = (
            grads
            if summed is None
            else tuple((earlier + latest for earlier, latest in zip(summed, grads)))
        )
    gradient_shard = reduce_grads(summed, flat_width)
    square_sum, loss_sum = lax.psum(
        (jnp.sum(gradient_shard * gradient_shard), loss_local), ("dp", "head")
    )
    grad_norm = jnp.sqrt(square_sum)
    clipped = gradient_shard * (CLIP_NORM / jnp.maximum(grad_norm, CLIP_NORM))
    shard_len = master.shape[1]
    flat_index = lax.axis_index("dp") * shard_len + jnp.arange(shard_len, dtype=jnp.int32)[None, :]
    width_head = D // head_total
    units_head = FF // head_total
    vector_start = (
        VOCAB // head_total * D
        + LAYERS * (3 * D * width_head + width_head * D + 2 * D * units_head)
        + (LEN + 2) * width_head
    )
    matrix_part = flat_index < vector_start
    step_rate = jnp.where(matrix_part, RATE_MATRIX, RATE_VECTOR)
    decay_rate = jnp.where(matrix_part, WEIGHT_DECAY, 0.0)
    new_first = BETA_ONE * first_moment + (1.0 - BETA_ONE) * clipped
    new_second = BETA_TWO * second_moment + (1.0 - BETA_TWO) * clipped * clipped
    adam_step = (
        new_first
        / (1.0 - BETA_ONE**STEP)
        / (jnp.sqrt(new_second / (1.0 - BETA_TWO**STEP)) + ADAM_EPS)
    )
    new_master = master - step_rate * (adam_step + decay_rate * master)
    return (loss_sum, grad_norm, new_master, new_first, new_second, new_master.astype(jnp.bfloat16))


def solution(mesh):
    return jax.shard_map(
        local,
        mesh=mesh,
        in_specs=(
            P("head", "dp"),
            P("head", "dp"),
            P("head", "dp"),
            P("dp", None),
            P("dp", None),
            P("dp", None),
            P("dp", None),
            P("dp", None, None),
            P(None, None, "head"),
            P("dp", None, "head"),
        ),
        out_specs=(P(), P(), P("head", "dp"), P("head", "dp"), P("head", "dp"), P("head", "dp")),
        check_vma=False,
    )
```

profile of v0, /device:TPU:0, one launch (start us, length us, event | category | flops | bytes accessed | tf_op | source)
XLA Modules:
  0.0 1709.5 jit_solution(8612595096317023399)
XLA Ops:
  11.3 5.0 copy.114
  25.8 5.8 fusion.13
  31.7 5.8 fusion.12
  37.4 214.5 %all-gather.3.cloned.1.call-done = bf16[1,5412864]{1,0:T(2,128)(2,1)} async-done(((bf16[1,338304]{1,0:T(2,128)(2,1)}), bf16[1,5412864]{1,0:T(2,128)(2,1)}) %all-gather.3.cloned.1.call-update) | async-done | bytes 10825744 | tf_op jit(solution)/shard_map/all_gather | solution.py:420
  259.8 202.0 %slice_reduce_fusion = bf16[4761432]{0:T(1024)(128)(2,1)} fusion(bf16[1,5412864]{1,0:T(2,128)(2,1)} %all-gather.3.cloned.1.call-done), kind=kLoop, calls=%fused_computation.20 | loop fusion | bytes 19045728 | tf_op jit(solution)/shard_map/slice | solution.py:71
  461.8 26.3 %reshape.1488 = bf16[15261,312]{1,0:T(8,128)(2,1)} reshape(bf16[4761432]{0:T(1024)(128)(2,1)} %slice_reduce_fusion) | data formatting | bytes 19045728 | tf_op jit(solution)/shard_map/reshape | solution.py:71
  488.1 7.6 gather_fusion
  496.7 12.0 reduce-scatter.21.cloned.1.call-start
  511.0 7.6 gather_fusion.4
  518.9 7.1 slice_reduce_fusion.3
  533.5 4.8 reduce-scatter.21.cloned.1.call-done
  565.7 9.1 slice_reduce_fusion.1
  589.2 4.2 multiply_convert_fusion.4
  596.6 10.8 reduce-scatter.25.cloned.1.call-done
  612.8 10.1 fusion.167
  626.6 8.6 fusion.166
  638.3 4.5 fusion.33
  646.0 8.2 fusion.139
  658.2 7.4 fusion.141
  670.0 11.3 fusion.140
  681.4 16.1 convolution_add_fusion
  697.5 22.2 %copy.136 = f32[15261,312]{1,0:T(8,128)} copy(f32[15261,312]{0,1:T(8,128)} %convolution_add_fusion) | data formatting | bytes 38091456 | tf_op jit(solution)/shard_map/add.7
  761.1 9.0 multiply_reduce_fusion
  781.5 8.8 multiply_reduce_fusion.1
  814.3 9.9 reduce-scatter.37.cloned.1.call-done
  844.5 22.2 %scatter_fusion = f32[15261,312]{1,0:T(8,128)} fusion(f32[15261,312]{1,0:T(8,128)} %copy.136, s32[1024]{0:T(1024)S(1)} %bitcast.306, f32[1024,312]{1,0:T(8,128)S(1)} %copy.137), kind=kCustom, calls=%fused_computation.10 | custom fusion | flops 319488 | bytes 3837952 | tf_op jit(solution)/shard_map/add | solution.py:459
  866.7 29.6 %reshape.1513 = f32[4761432]{0:T(1024)} reshape(f32[15261,312]{1,0:T(8,128)} %scatter_fusion) | data formatting | bytes 38091456 | tf_op jit(solution)/shard_map/reshape | solution.py:389
  898.2 164.0 %concatenate.51 = f32[5412864]{0:T(1024)} concatenate(f32[4761432]{0:T(1024)} %reshape.1513, f32[146016]{0:T(1024)S(1)} %copy-done.25, f32[48672]{0:T(1024)S(1)} %reshape.1515, f32[187200]{0:T(1024)S(1)} %copy-done.18, f32[187200]{0:T(1024)S(1)} %copy-done.17, f32[81432]{0:T(1024)S(1)} %reshape.1523, f32[312]{0:T(512)S(1)} %add.658, f32[600]{0:T(1024)S(1)} %copy-done.87), dimensions={0} | concatenate | bytes 43302912 | tf_op jit(solution)/shard_map/concatenate | solution.py:402
  1067.9 576.0 %all-reduce.10.cloned.1.call-done = f32[1,5412864]{1,0:T(1,128)} async-done(((f32[1,5412864]{1,0:T(1,128)}), f32[1,5412864]{1,0:T(1,128)}) %all-reduce.10.cloned.1.call-update) | async-done | bytes 21651472
  1643.8 4.5 multiply_reduce_fusion.6
  1648.3 39.6 %all-reduce.2 = (f32[]{:T(128)}, f32[]{:T(128)}) all-reduce(f32[]{:T(128)S(6)} %add.633, f32[]{:T(128)} %multiply_reduce_fusion.6), channel_id=1, replica_groups=mesh['dp'=16,'head'=2] {'dp','head'}, use_global_device_ids=true, to_apply=%region_56.57 | all-reduce | flops 2 | bytes 16 | tf_op jit(solution)/shard_map/psum | solution.py:462
  1688.7 12.7 fusion.142
  (573 shorter events, 199.4 us)
Async XLA Ops:
  7.2 244.7 %all-gather.3.cloned.1.call-start = ((), (), s32[]{:S(2)}) async-start(), calls=%async_computation.12 | async-start | bytes 23004672 | tf_op jit(solution)/shard_map/all_gather | solution.py:420
  10.9 521.5 %reduce-scatter.15.cloned.1.call-start = ((), (), s32[]{:S(2)}) async-start(), calls=%async_computation.13 | async-start | bytes 479232 | tf_op jit(solution)/shard_map/reduce_scatter | solution.py:287
  21.4 474.5 %copy-start.110 = (pred[512]{0:T(512)(128)(4,1)}, pred[512]{0:T(512)(128)(4,1)S(1)}, u32[]{:S(2)}) copy-start(pred[512]{0:T(512)(128)(4,1)S(1)} %get-tuple-element.60) | copy-start | bytes 1540
  21.4 510.0 %copy-start.112 = (pred[512]{0:T(512)(128)(4,1)}, pred[512]{0:T(512)(128)(4,1)S(1)}, u32[]{:S(2)}) copy-start(pred[512]{0:T(512)(128)(4,1)S(1)} %get-tuple-element.59) | copy-start | bytes 1540
  496.7 41.6 %reduce-scatter.21.cloned.1.call-start = ((), (), s32[]{:S(2)}) async-start(), calls=%async_computation.16 | async-start | bytes 479232 | tf_op jit(solution)/shard_map/reduce_scatter | solution.py:287
  531.4 46.5 %copy-start.53 = (f32[312]{0:T(512)}, f32[312]{0:T(512)S(1)}, u32[]{:S(2)}) copy-start(f32[312]{0:T(512)S(1)} %get-tuple-element.30) | copy-start | bytes 3748
  531.4 48.0 %copy-start.55 = (f32[312]{0:T(512)}, f32[312]{0:T(512)S(1)}, u32[]{:S(2)}) copy-start(f32[312]{0:T(512)S(1)} %get-tuple-element.27) | copy-start | bytes 3748
  531.4 48.0 %copy-start.85 = (f32[312]{0:T(512)}, f32[312]{0:T(512)S(1)}, u32[]{:S(2)}) copy-start(f32[312]{0:T(512)S(1)} %get-tuple-element.26) | copy-start | bytes 3748
  532.2 45.7 %reduce-scatter.17.cloned.1.call-start = ((), (), s32[]{:S(2)}) async-start(), calls=%async_computation.14 | async-start | bytes 479232 | tf_op jit(solution)/shard_map/reduce_scatter | solution.py:38
  533.4 44.5 %copy-start.2 = (f32[256,312]{0,1:T(8,128)}, f32[256,312]{0,1:T(8,128)S(1)}, u32[]{:S(2)}) copy-start(f32[256,312]{0,1:T(8,128)S(1)} %get-tuple-element.116) | copy-start | bytes 958468
  533.4 44.5 %copy-start.65 = (f32[256]{0:T(256)}, f32[256]{0:T(256)S(1)}, u32[]{:S(2)}) copy-start(f32[256]{0:T(256)S(1)} %broadcast_multiply_fusion.17) | copy-start | bytes 3076
  533.5 44.4 %copy-start.73 = (f32[256]{0:T(256)}, f32[256]{0:T(256)S(1)}, u32[]{:S(2)}) copy-start(f32[256]{0:T(256)S(1)} %add_rsqrt_fusion.5) | copy-start | bytes 3076
  539.3 38.6 %copy-start.4 = (f32[256,312]{0,1:T(8,128)}, f32[256,312]{0,1:T(8,128)S(1)}, u32[]{:S(2)}) copy-start(f32[256,312]{0,1:T(8,128)S(1)} %get-tuple-element.108) | copy-start | bytes 958468
  539.3 38.6 %copy-start.67 = (f32[256]{0:T(256)}, f32[256]{0:T(256)S(1)}, u32[]{:S(2)}) copy-start(f32[256]{0:T(256)S(1)} %broadcast_multiply_fusion.14) | copy-start | bytes 3076
  539.4 38.5 %copy-start.75 = (f32[256]{0:T(256)}, f32[256]{0:T(256)S(1)}, u32[]{:S(2)}) copy-start(f32[256]{0:T(256)S(1)} %add_rsqrt_fusion.2) | copy-start | bytes 3076
  553.5 42.5 %copy-start.58 = (f32[6,512]{1,0:T(8,128)}, f32[6,512]{1,0:T(8,128)S(1)}, u32[]{:S(2)}) copy-start(f32[6,512]{1,0:T(8,128)S(1)} %fusion.5) | copy-start | bytes 36868
  555.8 22.1 %reduce-scatter.23.cloned.1.call-start = ((), (), s32[]{:S(2)}) async-start(), calls=%async_computation.17 | async-start | bytes 479232 | tf_op jit(solution)/shard_map/reduce_scatter | solution.py:38
  564.6 32.0 %reduce-scatter.19.cloned.1.call-start = ((), (), s32[]{:S(2)}) async-start(), calls=%async_computation.15 | async-start | bytes 479232 | tf_op jit(solution)/shard_map/reduce_scatter | solution.py:38
  579.2 28.1 %copy-start.69 = (f32[256]{0:T(256)}, f32[256]{0:T(256)S(1)}, u32[]{:S(2)}) copy-start(f32[256]{0:T(256)S(1)} %broadcast_multiply_fusion.16) | copy-start | bytes 3076
  579.3 28.1 %copy-start.77 = (f32[256]{0:T(256)}, f32[256]{0:T(256)S(1)}, u32[]{:S(2)}) copy-start(f32[256]{0:T(256)S(1)} %add_rsqrt_fusion.4) | copy-start | bytes 3076
  587.1 20.3 %reduce-scatter.25.cloned.1.call-start = ((), (), s32[]{:S(2)}) async-start(), calls=%async_computation.18 | async-start | bytes 479232 | tf_op jit(solution)/shard_map/reduce_scatter | solution.py:38
  594.7 125.0 %reduce-scatter.33.cloned.1.call-start = ((), (), s32[]{:S(2)}) async-start(), calls=%async_computation.22 | async-start | bytes 479232 | tf_op jit(solution)/shard_map/reduce_scatter | solution.py:48
  669.7 51.2 %reduce-scatter.27.cloned.1.call-start = ((), (), s32[]{:S(2)}) async-start(), calls=%async_computation.19 | async-start | bytes 479232 | tf_op jit(solution)/shard_map/reduce_scatter | solution.py:48
  681.4 68.9 %reduce-scatter.35.cloned.1.call-start = ((), (), s32[]{:S(2)}) async-start(), calls=%async_computation.23 | async-start | bytes 479232 | tf_op jit(solution)/shard_map/reduce_scatter | solution.py:48
  730.6 21.6 %reduce-scatter.29.cloned.1.call-start = ((), (), s32[]{:S(2)}) async-start(), calls=%async_computation.20 | async-start | bytes 479232 | tf_op jit(solution)/shard_map/reduce_scatter | solution.py:48
  740.6 72.4 %reduce-scatter.31.cloned.1.call-start = ((), (), s32[]{:S(2)}) async-start(), calls=%async_computation.21 | async-start | bytes 479232 | tf_op jit(solution)/shard_map/reduce_scatter | solution.py:48
  804.0 20.2 %reduce-scatter.37.cloned.1.call-start = ((), (), s32[]{:S(2)}) async-start(), calls=%async_computation.24 | async-start | bytes 479232 | tf_op jit(solution)/shard_map/reduce_scatter | solution.py:48
  806.4 89.9 %all-reduce.8.cloned.1.call-start = ((), (), s32[]{:S(2)}) async-start(), calls=%async_computation.25 | async-start | bytes 811008
  839.1 804.7 %all-reduce.10.cloned.1.call-start = ((), (), s32[]{:S(2)}) async-start(), calls=%async_computation.26 | async-start | bytes 43302912
  866.7 31.4 %copy-start.25 = (f32[146016]{0:T(1024)S(1)}, f32[146016]{0:T(1024)}, u32[]{:S(2)}) copy-start(f32[146016]{0:T(1024)} %reshape.1514) | copy-start | bytes 1752196
  1062.2 626.5 %copy-start.30 = (f32[1,338304]{1,0:T(1,128)S(1)}, f32[1,338304]{1,0:T(1,128)}, u32[]{:S(2)}) copy-start(f32[1,338304]{1,0:T(1,128)} %param.11) | copy-start | bytes 4059652
  1062.2 626.4 %copy-start.8 = (f32[1,338304]{1,0:T(1,128)S(1)}, f32[1,338304]{1,0:T(1,128)}, u32[]{:S(2)}) copy-start(f32[1,338304]{1,0:T(1,128)} %param.10) | copy-start | bytes 4059652
  (129 other events, 812.3 us)
Sparse Core Ops, SparseCore 0:
  11.3 240.5 all-gather.2
  496.8 5.8 reduce-scatter.14
  532.4 5.9 reduce-scatter.20
  555.9 8.8 reduce-scatter.16
  567.6 8.8 reduce-scatter.22
  587.2 8.8 reduce-scatter.18
  598.5 8.8 reduce-scatter.24
  669.9 8.8 reduce-scatter.32
  681.5 8.8 reduce-scatter.26
  730.7 8.8 reduce-scatter.34
  742.5 8.8 reduce-scatter.28
  804.1 8.8 reduce-scatter.30
  815.3 8.8 reduce-scatter.36
  839.3 19.6 all-reduce.7
  1062.4 581.4 all-reduce.9
where the time goes:
time: 1730 us; the launch traced here: 1710 us
  waiting for transfers between devices  820 us (47%)
  local copies, waits for them, and re-layouts  524 us (30%)
  matrix products  147 us (8%)
  other arithmetic  109 us (6%)
  blocking collectives  73.2 us (4%)
  between operations  22.6 us (1%)
    unnamed x17, waiting for transfers between devices  576 us
    slice x5, local copies, waits for them, and re-layouts, unpack(): result.append(flat_weights[offset:offset + length].reshape(piece_shape))  222 us
    all_gather x1, waiting for transfers between devices, local(): lax.all_gather(master.astype(jnp.bfloat16), 'dp', axis=1, tiled=True)[0]  214 us
    concatenate x1, local copies, waits for them, and re-layouts, reduce_grads(): jnp.concatenate(members + [jnp.zeros((flat_width - used_count,), jnp.floa...  164 us
    psum x1, blocking collectives, local(): lax.psum((jnp.sum(gradient_shard * gradient_shard), loss_local), ('dp', '...  39.6 us
    reshape x6, local copies, waits for them, and re-layouts, reduce_grads(): member.reshape(-1)  35.4 us
  transfers between devices with their start and end apart: 15, of which 6 were waited for; matrix products, arithmetic and copies ran while one was open for 12% of the time, Pallas kernels for 0%

commit v1 on v0

v1 whole, which is shorter than its diff:
```python
import functools

import jax
import jax.numpy as jnp
from jax import lax
from jax.experimental import pallas as pl
from jax.experimental.pallas import tpu as pltpu
from jax.sharding import PartitionSpec as P

D = 312
HEADS = 12
HD = 26
HP = 32
FF = 1200
VOCAB = 30522
THD = 64
LEN = 512
STEP = 10
SROWS = 522

ATT_WEIGHT = 1.0
SOFTEN_FACTOR = 2.0
CLIP_NORM = 1.0
BETA_ONE = 0.9
BETA_TWO = 0.999
RATE_MATRIX = 0.06
RATE_VECTOR = 0.6
WEIGHT_DECAY = 0.01
ADAM_EPS = 1e-08
NORM_EPS = 1e-12
MASKED = -1000000000.0

F32 = jnp.float32
BF16 = jnp.bfloat16
LANES = 128
BOTH = ("dp", "head")
VMEM_BYTES = 56 * 1024 * 1024


def ceil_to(value, unit):
    return -(-value // unit) * unit


def call(kernel, out_shape, *args, scratch=(), smem=0):
    in_specs = [
        pl.BlockSpec(memory_space=pltpu.SMEM if index < smem else pltpu.VMEM)
        for index in range(len(args))
    ]
    out_specs = jax.tree.map(lambda _: pl.BlockSpec(memory_space=pltpu.VMEM), out_shape)
    return pl.pallas_call(
        kernel,
        out_shape=out_shape,
        in_specs=in_specs,
        out_specs=out_specs,
        scratch_shapes=list(scratch),
        compiler_params=pltpu.CompilerParams(vmem_limit_bytes=VMEM_BYTES),
    )(*args)


class Plan:
    def __init__(self, n, m, share):
        self.n, self.m, self.share = n, m, share
        self.rows_share = share // LANES
        self.vocab = VOCAB // m
        self.width = D // m
        self.units = FF // m
        self.first = [min(-(-d * share // D), self.vocab) for d in range(n + 1)]
        widest = -(-share // D)
        self.rows = ceil_to(widest + 3, 16)
        table = self.vocab * D
        self.table = table
        self.tail_row = table // LANES
        self.tail_off = table % LANES
        self.tail_rows = n * self.rows_share - self.tail_row
        self.tail_pad = ceil_to(self.tail_rows + 40, 16)
        w, u = self.width, self.units
        self.pieces = []
        base = self.tail_off
        for rows, wide in ((3 * D, w), (w, D), (D, u), (u, D), (SROWS, w), (m, w), (1, u)):
            self.pieces.append((base, wide, rows))
            base += rows * wide
        self.special = n == 16 and self.tail_row // self.rows_share == n - 2
        if self.special:
            self.low_rows = (n - 1) * self.rows_share - self.tail_row
            self.slice_rows = ceil_to(-(-self.rows_share // 8), 16)


def period(width):
    step = 16
    while step * width % LANES:
        step *= 2
    return step, step * width // LANES


def rows_at(start, count, stride):
    return pl.ds(start, count) if count == 1 else pl.ds(start, count, stride=stride)


def spread_rows(src, dst, base, width, rows):
    step, lane_rows = period(width)
    tiles = -(-width // LANES)
    for phase in range(min(step, rows)):
        count = len(range(phase, rows, step))
        line, off = divmod(base + phase * width, LANES)
        loaded = [
            src[rows_at(line + j, count, lane_rows), :] for j in range(tiles + (1 if off else 0))
        ]
        lane = lax.broadcasted_iota(jnp.int32, (count, LANES), 1)
        for tile in range(tiles):
            value = loaded[tile]
            if off:
                value = jnp.where(
                    lane < LANES - off,
                    pltpu.roll(value, LANES - off, 1),
                    pltpu.roll(loaded[tile + 1], LANES - off, 1),
                )
            dst[tile, rows_at(phase, count, step), :] = value


def pack_rows(src, dst, base, width, rows):
    step, lane_rows = period(width)
    tiles = -(-width // LANES)
    for phase in range(min(step, rows)):
        count = len(range(phase, rows, step))
        line, off = divmod(base + phase * width, LANES)
        loaded = [
            src[tile, rows_at(phase, count, step), :] for tile in range(tiles)
        ]
        lane = lax.broadcasted_iota(jnp.int32, (count, LANES), 1)
        rolled = [pltpu.roll(value, off, 1) if off else value for value in loaded]
        for j in range(-(-(off + width) // LANES)):
            value = jnp.zeros((count, LANES), F32)
            if j < tiles:
                value = jnp.where(lane >= off, rolled[j], value)
            if off and j > 0:
                value = jnp.where(lane < off, rolled[j - 1], value)
            at = rows_at(line + j, count, lane_rows)
            dst[at, :] = dst[at, :] + value


def column_tiles(width):
    return [(t, t * LANES, min(LANES, width - t * LANES)) for t in range(-(-width // LANES))]


def shift_lines(source, count, start, max_line):
    low, high = start // LANES, lax.rem(start, LANES)
    first = source[0:count, :]
    second = source[1 : count + 1, :]
    for line in range(1, max_line + 1):
        first = jnp.where(low == line, source[line : count + line, :], first)
        second = jnp.where(low == line, source[line + 1 : count + line + 1, :], second)
    lane = lax.broadcasted_iota(jnp.int32, (count, LANES), 1)
    back = lax.rem(LANES - high, LANES)
    return jnp.where(lane < LANES - high, pltpu.roll(first, back, 1), pltpu.roll(second, back, 1))


def table_rows_kernel(plan, place, chunk, after, out, joined, shifted, rows):
    share = plan.rows_share
    lines = joined.shape[0]
    joined[share & -8 :, :] = jnp.zeros((lines - (share & -8), LANES), F32)
    joined[0:share, :] = chunk[...]
    joined[share : share + 8, :] = after[...]
    shifted[...] = jnp.zeros_like(shifted)
    shifted[0 : share + 1, :] = shift_lines(joined, share + 1, place[0], 2)
    spread_rows(shifted, rows, 0, D, plan.rows)
    row = lax.broadcasted_iota(jnp.int32, (plan.rows, LANES), 0)
    for tile, left, wide in column_tiles(D):
        value = jnp.where(row < place[1], rows[tile], 0.0).astype(BF16)
        out[:, left : left + wide] = value[:, 0:wide]


def table_rows(plan, place, chunk, after):
    lines = ceil_to(max(plan.rows_share + 16, plan.rows // 16 * 39 + 2), 8)
    return call(
        functools.partial(table_rows_kernel, plan),
        jax.ShapeDtypeStruct((plan.rows, D), BF16),
        place,
        chunk,
        after,
        scratch=[
            pltpu.VMEM((lines, LANES), F32),
            pltpu.VMEM((lines, LANES), F32),
            pltpu.VMEM((3, plan.rows, LANES), F32),
        ],
        smem=1,
    )


def table_pack_kernel(plan, place, grads, before, out, rows, lines):
    rows[...] = jnp.zeros_like(rows)
    for tile, left, wide in column_tiles(D):
        rows[tile, 16 : 16 + plan.rows, 0:wide] = grads[:, left : left + wide]
        rows[tile, 15:16, 0:wide] = before[0:1, left : left + wide]
    lines[...] = jnp.zeros_like(lines)
    pack_rows(rows, lines, 0, D, plan.rows + 16)
    count = plan.rows_share
    start = 39 * LANES - place[0]
    low, high = start // LANES - 36, lax.rem(start, LANES)
    first = lines[36 : 36 + count, :]
    second = lines[37 : 37 + count, :]
    for line in range(1, 4):
        first = jnp.where(low == line, lines[36 + line : 36 + line + count, :], first)
        second = jnp.where(low == line, lines[37 + line : 37 + line + count, :], second)
    lane = lax.broadcasted_iota(jnp.int32, (count, LANES), 1)
    back = lax.rem(LANES - high, LANES)
    out[...] = jnp.where(
        lane < LANES - high, pltpu.roll(first, back, 1), pltpu.roll(second, back, 1)
    )


def table_pack(plan, place, grads, before):
    lines = ceil_to(max(plan.rows_share + 48, (plan.rows // 16 + 1) * 39 + 2), 8)
    return call(
        functools.partial(table_pack_kernel, plan),
        jax.ShapeDtypeStruct((plan.rows_share, LANES), F32),
        place,
        grads,
        before,
        scratch=[
            pltpu.VMEM((3, plan.rows + 16, LANES), F32),
            pltpu.VMEM((lines, LANES), F32),
        ],
        smem=1,
    )


def unpack_kernel(plan, tail, *refs):
    outs, (lines, wide) = refs[:-2], refs[-2:]
    lines[...] = tail[0].astype(F32)
    for out, (base, width, rows) in zip(outs, plan.pieces):
        spread_rows(lines, wide, base, width, rows)
        for tile, left, part in column_tiles(width):
            out[0, :, left : left + part] = wide[tile, 0:rows, 0:part].astype(BF16)


def unpack_tail(plan, tail):
    m = tail.shape[0]
    shapes = [jax.ShapeDtypeStruct((m, rows, width), BF16) for _, width, rows in plan.pieces]
    tallest = max(rows for _, _, rows in plan.pieces)
    widest = max(-(-width // LANES) for _, width, _ in plan.pieces)
    return pl.pallas_call(
        functools.partial(unpack_kernel, plan),
        out_shape=shapes,
        grid=(m,),
        in_specs=[pl.BlockSpec((1,) + tail.shape[1:], lambda i: (i, 0, 0))],
        out_specs=[pl.BlockSpec((1,) + s.shape[1:], lambda i: (i, 0, 0)) for s in shapes],
        scratch_shapes=[
            pltpu.VMEM(tail.shape[1:], F32),
            pltpu.VMEM((widest, tallest, LANES), F32),
        ],
        compiler_params=pltpu.CompilerParams(vmem_limit_bytes=VMEM_BYTES),
    )(tail)


def pack_kernel(plan, *refs):
    ins, out, (wide, lines) = refs[:-3], refs[-3], refs[-2:]
    lines[...] = jnp.zeros_like(lines)
    for source, (base, width, rows) in zip(ins, plan.pieces):
        for tile, left, part in column_tiles(width):
            if part < LANES:
                wide[tile, 0:rows, :] = jnp.zeros((rows, LANES), F32)
            wide[tile, 0:rows, 0:part] = source[0, :, left : left + part]
        pack_rows(wide, lines, base, width, rows)
    out[0] = lines[...]


def pack_tail(plan, pieces):
    m = pieces[0].shape[0]
    tallest = max(rows for _, _, rows in plan.pieces)
    widest = max(-(-width // LANES) for _, width, _ in plan.pieces)
    return pl.pallas_call(
        functools.partial(pack_kernel, plan),
        out_shape=jax.ShapeDtypeStruct((m, plan.tail_pad, LANES), F32),
        grid=(m,),
        in_specs=[pl.BlockSpec((1,) + p.shape[1:], lambda i: (i, 0, 0)) for p in pieces],
        out_specs=pl.BlockSpec((1, plan.tail_pad, LANES), lambda i: (i, 0, 0)),
        scratch_shapes=[
            pltpu.VMEM((widest, tallest, LANES), F32),
            pltpu.VMEM((plan.tail_pad, LANES), F32),
        ],
        compiler_params=pltpu.CompilerParams(vmem_limit_bytes=VMEM_BYTES),
    )(*pieces)


def swap(value, axis, bit, size):
    return lax.ppermute(value, axis, [(i, i ^ bit) for i in range(size)])


def gather_to_all(value, plan):
    return lax.all_to_all(
        jnp.broadcast_to(value[None], (plan.n,) + value.shape), "dp", 0, 0, tiled=False
    )


def join_heads(value, head, m):
    if m != 2:
        return lax.all_gather(value, "head", axis=0, tiled=False)
    other = swap(value, "head", 1, m)
    mine_first = head == 0
    return jnp.stack([jnp.where(mine_first, value, other), jnp.where(mine_first, other, value)])


def total_all(value, plan):
    if plan.n & (plan.n - 1) or plan.m & (plan.m - 1):
        return lax.psum(value, BOTH)
    bit = 1
    while bit < plan.m:
        value = value + swap(value, "head", bit, plan.m)
        bit *= 2
    bit = 1
    while bit < plan.n:
        value = value + swap(value, "dp", bit, plan.n)
        bit *= 2
    return value


def gather_tail(plan, chunk):
    n, share = plan.n, plan.rows_share
    if not plan.special:
        whole = lax.all_gather(chunk, "dp", axis=0, tiled=True)
        tail = whole[plan.tail_row :]
        return jnp.pad(tail, ((0, plan.tail_pad - plan.tail_rows), (0, 0)))
    d = lax.axis_index("dp")
    low, size = plan.low_rows, plan.slice_rows
    padded = jnp.pad(chunk, ((0, 8 * size - share), (0, 0)))
    from_low = jnp.pad(chunk[share - low :], ((0, 8 * size - low), (0, 0)))
    own = jnp.where(d == n - 2, from_low, padded)
    mine = own[7 * size :]
    for k in range(7):
        part = lax.ppermute(
            own[k * size : (k + 1) * size], "dp", [(n - 2, 2 * k), (n - 1, 2 * k + 1)]
        )
        mine = jnp.where(d // 2 == k, part, mine)
    slices = gather_to_all(mine, plan)
    low_part = slices[0::2].reshape(8 * size, LANES)[:low]
    high_part = slices[1::2].reshape(8 * size, LANES)[:share]
    return jnp.pad(
        jnp.concatenate([low_part, high_part]), ((0, plan.tail_pad - plan.tail_rows), (0, 0))
    )


def reduce_tail(plan, tail):
    n, share = plan.n, plan.rows_share
    d = lax.axis_index("dp")
    if not plan.special:
        total = lax.psum(tail, "dp")
        front = jnp.zeros((share, LANES), F32)
        start = jnp.clip(d * share - plan.tail_row + share, 0, plan.tail_pad)
        return lax.dynamic_slice_in_dim(
            jnp.concatenate([front, total[: plan.tail_rows], front]), start, share
        )
    low, size = plan.low_rows, plan.slice_rows
    low_part = jnp.pad(tail[:low], ((0, 8 * size - low), (0, 0))).reshape(8, size, LANES)
    high_part = jnp.pad(tail[low : low + share], ((0, 8 * size - share), (0, 0)))
    both = jnp.stack([low_part, high_part.reshape(8, size, LANES)], axis=1)
    parts = lax.all_to_all(
        both.reshape(n, size, LANES).astype(BF16), "dp", 0, 0, tiled=False
    )
    mine = jnp.sum(parts.astype(F32), axis=0)
    whole = []
    for k in range(7):
        whole.append(lax.ppermute(mine, "dp", [(2 * k, n - 2), (2 * k + 1, n - 1)]))
    whole = jnp.concatenate(whole + [mine])
    for_low = jnp.pad(whole[:low], ((share - low, 0), (0, 0)))
    return jnp.where(d == n - 2, for_low, jnp.where(d == n - 1, whole[:share], 0.0))


def attention_kernel(proj, teacher, sent_col, sent_row, weight, plain, grad_q, grad_k, loss):
    @pl.when(pl.program_id(0) == 0)
    def _():
        loss[...] = jnp.zeros_like(loss)

    allowed = sent_col[...] == sent_row[...]

    def probs(queries, key_heads, scale):
        scores = lax.dot_general(
            queries, key_heads, (((0,), (0,)), ((), ())), preferred_element_type=F32
        )
        scores = jnp.where(allowed, scores * scale, MASKED)
        exponent = jnp.exp(scores - jnp.max(scores, axis=-1, keepdims=True))
        return exponent * (1.0 / jnp.sum(exponent, axis=-1, keepdims=True))

    teacher_prob = probs(teacher[0, 0], teacher[1, 0], THD ** (-0.5))
    queries, key_heads = proj[0, 0], proj[1, 0]
    prob = probs(queries, key_heads, HD ** (-0.5))
    gap = (prob - teacher_prob) * weight[...]
    loss[...] += jnp.sum(gap * gap, axis=0, keepdims=True) * ATT_WEIGHT
    pulled = prob * gap
    inner = jnp.sum(pulled, axis=-1, keepdims=True)
    grad_scores = (
        (pulled - prob * inner) * (plain[...] * (2.0 * ATT_WEIGHT))
    ).astype(BF16)
    grad_q[0] = lax.dot_general(
        key_heads, grad_scores, (((1,), (1,)), ((), ())), preferred_element_type=F32
    )
    grad_k[0] = lax.dot_general(
        queries, grad_scores, (((1,), (0,)), ((), ())), preferred_element_type=F32
    )


def map_attention(proj, teacher, sent_col, sent_row, weight, plain):
    whole = lambda i: (0, 0)
    return pl.pallas_call(
        attention_kernel,
        out_shape=[
            jax.ShapeDtypeStruct((HEADS, HP, LEN), F32),
            jax.ShapeDtypeStruct((HEADS, HP, LEN), F32),
            jax.ShapeDtypeStruct((1, LEN), F32),
        ],
        grid=(HEADS,),
        in_specs=[
            pl.BlockSpec((3, 1, HP, LEN), lambda i: (0, i, 0, 0)),
            pl.BlockSpec((2, 1, THD, LEN), lambda i: (0, i, 0, 0)),
            pl.BlockSpec((LEN, 1), whole),
            pl.BlockSpec((1, LEN), whole),
            pl.BlockSpec((LEN, 1), whole),
            pl.BlockSpec((LEN, 1), whole),
        ],
        out_specs=[
            pl.BlockSpec((1, HP, LEN), lambda i: (i, 0, 0)),
            pl.BlockSpec((1, HP, LEN), lambda i: (i, 0, 0)),
            pl.BlockSpec((1, LEN), whole),
        ],
        compiler_params=pltpu.CompilerParams(vmem_limit_bytes=VMEM_BYTES),
    )(proj, teacher, sent_col, sent_row, weight, plain)


def dot(spec, left, right, **options):
    return jnp.einsum(spec, left, right, preferred_element_type=F32, **options)


def one_hot(index, size):
    return (index[:, None] == jnp.arange(size, dtype=jnp.int32)[None, :]).astype(BF16)


def exact_dot(left, right, spec):
    high = right.astype(BF16)
    rest = right - high.astype(F32)
    middle = rest.astype(BF16)
    low = (rest - middle.astype(F32)).astype(BF16)
    return dot(spec, left, high) + dot(spec, left, middle) + dot(spec, left, low)


def norm_forward(value, gain_row, bias_row):
    centred = value - jnp.mean(value, axis=-1, keepdims=True)
    inverse = lax.rsqrt(jnp.mean(centred * centred, axis=-1, keepdims=True) + NORM_EPS)
    normed = centred * inverse
    return (normed * gain_row + bias_row, (normed, inverse))


def norm_backward(gradient, saved, gain_row):
    normed, inverse = saved
    scaled = gradient * gain_row
    inner_part = (
        scaled
        - jnp.mean(scaled, -1, keepdims=True)
        - normed * jnp.mean(scaled * normed, -1, keepdims=True)
    )
    return (inner_part * inverse, jnp.sum(gradient * normed, 0), jnp.sum(gradient, 0))


def masked_softmax(scores, allowed):
    scores = jnp.where(allowed, scores, MASKED)
    exponent = jnp.exp(scores - jnp.max(scores, axis=-1, keepdims=True))
    return exponent / jnp.sum(exponent, axis=-1, keepdims=True)


def local(
    master,
    first_moment,
    second_moment,
    token_ids,
    token_types,
    counts,
    mask_pos,
    teacher_states,
    teacher_qk,
    mentor_logits,
):
    n, m = lax.axis_size("dp"), lax.axis_size("head")
    d, h = lax.axis_index("dp"), lax.axis_index("head")
    share_len = master.shape[1]
    assert share_len % LANES == 0 and token_ids.shape[0] == m
    plan = Plan(n, m, share_len)
    share = plan.rows_share
    devices = n * m
    slots = max(8, 1024 // devices)
    masks = mask_pos.shape[1]
    picks = devices * masks

    own_row = lambda value: lax.dynamic_index_in_dim(value, h, 0, keepdims=False)
    ids, types, sizes, pos = (own_row(v) for v in (token_ids, token_types, counts, mask_pos))

    vocab_head = ids // plan.vocab
    vocab_row = ids - vocab_head * plan.vocab
    owner = (vocab_row * D) // share_len * m + vocab_head
    order = jnp.arange(LEN, dtype=jnp.int32)
    same = ids[:, None] == ids[None, :]
    leader = jnp.min(jnp.where(same, order[None, :], LEN), axis=1)
    leads = leader == order
    rank = jnp.sum(
        (owner[:, None] == owner[None, :]) & leads[None, :] & (order[None, :] < leader[:, None]),
        axis=1,
        dtype=jnp.int32,
    )
    rounds_here = jnp.max(rank) // slots + 1

    def token_slots(turn):
        place = rank - turn * slots
        return jnp.where((place >= 0) & (place < slots), owner * slots + place, -1)

    def ask(turn, extra):
        slot = token_slots(turn)
        hit = jnp.arange(devices * slots, dtype=jnp.int32)[:, None] == slot[None, :]
        wanted = jnp.max(jnp.where(hit, vocab_row[None, :], -1), axis=1).reshape(devices, slots)
        sent = jnp.concatenate(
            [wanted, jnp.broadcast_to(extra, (devices, 1)).astype(jnp.int32)], axis=1
        )
        sent = jnp.pad(sent, ((0, 0), (0, ceil_to(slots + 1, LANES) - slots - 1)))
        got = lax.all_to_all(sent, BOTH, 0, 0, tiled=True)
        asked = got[:, :slots].reshape(-1)
        return asked, got[:, slots]

    first_row = jnp.minimum((d * share_len + D - 1) // D, plan.vocab)
    row_count = jnp.minimum(((d + 1) * share_len + D - 1) // D, plan.vocab) - first_row

    chunk = master.reshape(share, LANES)
    after = lax.ppermute(chunk[:8], "dp", [(i + 1, i) for i in range(n - 1)])
    place = jnp.stack([first_row * D - d * share_len, row_count]).astype(jnp.int32)
    place = jnp.where(row_count > 0, place, 0)
    words_own = table_rows(plan, place, chunk, after)

    def fetch(turn, asked):
        rows = dot(
            "sv,vd->sd", one_hot(jnp.where(asked >= 0, asked - first_row, -1), plan.rows), words_own
        ).astype(BF16)
        back = lax.all_to_all(
            rows.reshape(devices, slots, D), BOTH, 0, 0, tiled=True
        ).reshape(-1, D)
        return dot("ts,sd->td", one_hot(token_slots(turn), devices * slots), back)

    asked_first, needs = ask(0, rounds_here)
    rounds = jnp.max(needs)
    words = fetch(0, asked_first)
    words = lax.while_loop(
        lambda state: state[0] < rounds,
        lambda state: (
            state[0] + 1,
            state[1] + fetch(state[0], ask(state[0], rounds_here)[0]),
        ),
        (jnp.int32(1), words),
    )[1]

    tail_own = gather_tail(plan, chunk.astype(BF16))
    tail = join_heads(tail_own, h, m)
    attn_in, attn_out, ffn_in, ffn_out, shared_half, qv_bias, up_bias = unpack_tail(plan, tail)
    shared = jnp.concatenate([shared_half[i] for i in range(m)], axis=1).astype(F32)
    per_head = plan.width // HD
    spread = (
        (jnp.arange(plan.width) // HD * HP + jnp.arange(plan.width) % HD)[:, None]
        == jnp.arange(per_head * HP)[None, :]
    ).astype(BF16)
    attn_in = attn_in.reshape(m, 3, D, plan.width)
    wide_in = dot("hcde,ef->hcdf", attn_in, spread).astype(BF16)
    wide_out = dot("ef,hed->hfd", spread, attn_out).astype(BF16).reshape(m * per_head * HP, D)
    wide_bias = dot("hce,ef->chf", qv_bias, spread).reshape(2, 1, m * per_head * HP)
    qkv_bias = jnp.concatenate(
        [wide_bias[0], jnp.zeros_like(wide_bias[0]), wide_bias[1]]
    ).reshape(3, m, per_head * HP)

    mentor = mentor_logits.reshape(m * masks, plan.vocab)
    halved = mentor.astype(F32) / SOFTEN_FACTOR
    mentor_top = jnp.max(halved, axis=-1)
    mentor_sum = jnp.sum(jnp.exp(halved - mentor_top[:, None]), axis=-1)
    pairs = join_heads(jnp.stack([mentor_top, mentor_sum]), h, m)
    top = jnp.max(pairs[:, 0], axis=0)
    log_total = top + jnp.log(jnp.sum(pairs[:, 1] * jnp.exp(pairs[:, 0] - top), axis=0))
    part_a = log_total.astype(BF16)
    part_b = (log_total - part_a.astype(F32)).astype(BF16)
    part_c = (log_total - part_a.astype(F32) - part_b.astype(F32)).astype(BF16)
    blocks = []
    room = plan.rows - 3
    for owner_index in range(n):
        low = plan.first[owner_index]
        high = min(low + room, plan.vocab)
        blocks.append(jnp.pad(mentor[:, low:high], ((0, 0), (0, room - (high - low)))))
    blocks = jnp.stack(blocks)
    stats = jnp.stack([part_a, part_b, part_c], axis=-1)
    blocks = jnp.concatenate(
        [blocks, jnp.broadcast_to(stats[None], (n,) + stats.shape)], axis=-1
    )
    mentor_here = lax.all_to_all(blocks, "dp", 0, 0, tiled=False).reshape(picks, plan.rows)

    teacher_weight = join_heads(teacher_qk, h, m)
    states = own_row(teacher_states)
    teacher_proj = dot("hdce,ld->chel", teacher_weight, states).astype(BF16)
    teacher_proj = teacher_proj.reshape(2, HEADS, THD, LEN)

    ends = jnp.cumsum(sizes)
    passed = (order[:, None] >= ends[None, :]).astype(jnp.int32)
    sentence = jnp.sum(passed, axis=-1)
    within = order - jnp.sum(passed * sizes[None, :], axis=-1)
    valid = (sentence < sizes.shape[0] - 1).astype(F32)

    position_hot = one_hot(within, LEN)
    positions = dot("lp,pd->ld", position_hot, shared[:LEN].astype(BF16))
    type_row = jnp.where(types[:, None] == 0, shared[LEN], shared[LEN + 1])
    state_zero, saved_zero = norm_forward(
        words + positions + type_row, shared[LEN + 2], shared[LEN + 3]
    )
    gathered = state_zero.astype(BF16)
    shared_rows = shared[LEN + 4 :]
    proj = dot("hcdf,ld->chfl", wide_in, gathered) + qkv_bias[..., None]
    proj = proj.astype(BF16).reshape(3, HEADS, HP, LEN)

    pick_hot = one_hot(pos, LEN)
    picked_any = jnp.sum(pick_hot.astype(F32), axis=0) > 0
    plain = jnp.where(picked_any, 0.0, 1.0)
    grad_q, grad_k, map_rows = map_attention(
        proj,
        teacher_proj,
        sentence[:, None],
        sentence[None, :],
        valid[:, None],
        plain[:, None],
    )

    pick_sentence = jnp.sum(jnp.where(pos[:, None] == order[None, :], sentence[None, :], 0), 1)
    pick_allowed = (pick_sentence[:, None] == sentence[None, :])[None]
    pick_valid = (pick_sentence < sizes.shape[0] - 1).astype(F32)[None, :, None]
    queries, key_heads, values = proj[0], proj[1], proj[2]
    pick_q = dot("hel,pl->hpe", queries, pick_hot).astype(BF16)
    prob = masked_softmax(dot("hpe,hel->hpl", pick_q, key_heads) * HD ** (-0.5), pick_allowed)
    pick_tq = dot("hel,pl->hpe", teacher_proj[0], pick_hot).astype(BF16)
    pick_teacher = masked_softmax(
        dot("hpe,hel->hpl", pick_tq, teacher_proj[1]) * THD ** (-0.5), pick_allowed
    )
    prob_low = prob.astype(BF16)
    mixed = dot("hpl,hel->phe", prob_low, values).astype(BF16).reshape(masks, HEADS * HP)
    state_pick = exact_dot(pick_hot, state_zero, "pl,ld->pd")
    state_one, saved_one = norm_forward(
        state_pick + dot("pf,fd->pd", mixed, wide_out) + shared_rows[4],
        shared_rows[0],
        shared_rows[1],
    )
    state_one_low = state_one.astype(BF16)
    pre_act = dot("pd,hdu->hpu", state_one_low, ffn_in) + up_bias.astype(F32)
    hidden_act = jax.nn.gelu(pre_act, approximate=False).astype(BF16)
    state_two, saved_two = norm_forward(
        state_one + dot("hpu,hud->pd", hidden_act, ffn_out) + shared_rows[5],
        shared_rows[2],
        shared_rows[3],
    )

    chosen = join_heads(gather_to_all(state_two.astype(BF16), plan), h, m)
    chosen = jnp.swapaxes(chosen, 0, 1).reshape(picks, D)
    column_ok = jnp.arange(plan.rows, dtype=jnp.int32)[None, :] < row_count
    logits = dot("md,vd->mv", chosen, words_own) / SOFTEN_FACTOR
    logits = jnp.where(column_ok, logits, -1e30)
    local_top = jnp.max(logits, axis=-1)
    local_sum = jnp.sum(
        jnp.where(column_ok, jnp.exp(logits - local_top[:, None]), 0.0), axis=-1
    )
    pairs = join_heads(jnp.stack([local_top, local_sum]), h, m)
    top = jnp.max(pairs[:, 0], axis=0)
    total = jnp.sum(pairs[:, 1] * jnp.exp(pairs[:, 0] - top), axis=0)
    pairs = gather_to_all(jnp.stack([top, total]), plan)
    top = jnp.max(pairs[:, 0], axis=0)
    student_total = top + jnp.log(jnp.sum(pairs[:, 1] * jnp.exp(pairs[:, 0] - top), axis=0))
    mentor_f32 = mentor_here.astype(F32)
    mentor_total = mentor_f32[:, room] + mentor_f32[:, room + 1] + mentor_f32[:, room + 2]
    target = jnp.where(
        column_ok, jnp.exp(mentor_f32 / SOFTEN_FACTOR - mentor_total[:, None]), 0.0
    )
    student = jnp.where(column_ok, jnp.exp(logits - student_total[:, None]), 0.0)
    grad_logits = ((student - target) / SOFTEN_FACTOR).astype(BF16)
    cross = jnp.sum(jnp.where(column_ok, target * logits, 0.0))
    own_totals = lax.dynamic_slice_in_dim(student_total, (d * m + h) * masks, masks)
    loss_local = jnp.sum(map_rows) + jnp.sum(own_totals) - cross

    grad_chosen = dot("mv,vd->md", grad_logits, words_own).reshape(n, m, masks, D)
    if m == 2:
        mine = lax.dynamic_index_in_dim(grad_chosen, h, 1, keepdims=False)
        other = lax.dynamic_index_in_dim(grad_chosen, 1 - h, 1, keepdims=False)
        mine = mine + swap(other.astype(BF16), "head", 1, 2).astype(F32)
    else:
        mine = lax.psum_scatter(grad_chosen, "head", scatter_dimension=1, tiled=False)
    grad_pick = jnp.sum(
        lax.all_to_all(mine.astype(BF16), "dp", 0, 0, tiled=False).astype(F32), axis=0
    )

    repeats = pos[:, None] == pos[None, :]
    mask_order = jnp.arange(masks, dtype=jnp.int32)
    leads_pick = jnp.min(jnp.where(repeats, mask_order[None, :], masks), axis=1) == mask_order
    grad_pick = jnp.where(
        leads_pick[:, None], exact_dot(repeats.astype(BF16), grad_pick, "pq,qd->pd"), 0.0
    )
    grad_res, gain_two, bias_two = norm_backward(grad_pick, saved_two, shared_rows[2])
    grad_branch = grad_res.astype(BF16)
    grad_ffn_out = dot("hpu,pd->hud", hidden_act, grad_branch)
    grad_hidden = dot("pd,hud->hpu", grad_branch, ffn_out)
    _, gelu_pull = jax.vjp(lambda value: jax.nn.gelu(value, approximate=False), pre_act)
    grad_pre = gelu_pull(grad_hidden)[0].astype(BF16)
    grad_ffn_in = dot("pd,hpu->hdu", state_one_low, grad_pre)
    grad_up_bias = jnp.sum(grad_pre.astype(F32), 1, keepdims=True)
    grad_one = grad_res + dot("hpu,hdu->pd", grad_pre, ffn_in)
    grad_mid, gain_one, bias_one = norm_backward(grad_one, saved_one, shared_rows[0])
    grad_attended = grad_mid.astype(BF16)
    grad_attn_out = dot("pf,pd->fd", mixed, grad_attended).reshape(m, per_head * HP, D)
    grad_mixed = dot("pd,fd->pf", grad_attended, wide_out).astype(BF16)
    grad_mixed = grad_mixed.reshape(masks, HEADS, HP)
    grad_values = dot("hpl,phe->hel", prob_low, grad_mixed)
    grad_prob = dot("phe,hel->hpl", grad_mixed, values)
    grad_prob = grad_prob + 2.0 * ATT_WEIGHT * (prob - pick_teacher) * pick_valid
    grad_scores = prob * (grad_prob - jnp.sum(prob * grad_prob, -1, keepdims=True))
    grad_scores = jnp.where(leads_pick[None, :, None], grad_scores, 0.0).astype(BF16)
    pick_grad_q = dot("hpl,hel->hpe", grad_scores, key_heads) * HD ** (-0.5)
    grad_k = (grad_k + dot("hpl,hpe->hel", grad_scores, pick_q)) * HD ** (-0.5)
    grad_q = grad_q * HD ** (-0.5) + dot("hpe,pl->hel", pick_grad_q.astype(BF16), pick_hot)
    grad_proj = jnp.stack([grad_q, grad_k, grad_values]).astype(BF16)
    grad_proj = grad_proj.reshape(3, m, per_head * HP, LEN)
    narrow = dot("ef,chfl->chel", spread, grad_proj).astype(BF16)
    grad_attn_in = dot("ld,chel->hcde", gathered, narrow).reshape(m, 3 * D, plan.width)
    bias_sums = jnp.sum(narrow.astype(F32), axis=-1)
    grad_qv = jnp.stack([bias_sums[0], bias_sums[2]], axis=1)
    grad_in = dot("chfl,hcdf->ld", grad_proj, wide_in) + exact_dot(
        pick_hot, grad_mid, "pl,pd->ld"
    )
    grad_embed, gain_embed, bias_embed = norm_backward(grad_in, saved_zero, shared[LEN + 2])

    grad_positions = exact_dot(position_hot, grad_embed, "lp,ld->pd")
    type_one = jnp.sum(jnp.where(types[:, None] == 1, grad_embed, 0.0), axis=0)
    type_zero = jnp.sum(jnp.where(types[:, None] == 0, grad_embed, 0.0), axis=0)
    vectors = jnp.stack(
        [
            type_zero,
            type_one,
            gain_embed,
            bias_embed,
            gain_one,
            bias_one,
            gain_two,
            bias_two,
            jnp.sum(grad_mid, 0),
            jnp.sum(grad_res, 0),
        ]
    )
    grad_shared = jnp.concatenate([grad_positions, vectors]).reshape(SROWS, m, plan.width)
    grad_attn_out = exact_dot(spread, grad_attn_out, "ef,hfd->hed")

    word_grads = grad_embed.astype(BF16)

    def deliver(turn, asked):
        slot_grads = dot("ts,td->sd", one_hot(token_slots(turn), devices * slots), word_grads)
        got = lax.all_to_all(
            slot_grads.astype(BF16).reshape(devices, slots, D), BOTH, 0, 0, tiled=True
        ).reshape(-1, D)
        hot = one_hot(jnp.where(asked >= 0, asked - first_row, -1), plan.rows)
        return dot("sv,sd->vd", hot, got)

    grad_table = dot("mv,md->vd", grad_logits, chosen) + deliver(0, asked_first)
    grad_table = lax.while_loop(
        lambda state: state[0] < rounds,
        lambda state: (
            state[0] + 1,
            state[1] + deliver(state[0], ask(state[0], rounds_here)[0]),
        ),
        (jnp.int32(1), grad_table),
    )[1]
    last_row = lax.dynamic_slice_in_dim(grad_table, jnp.maximum(row_count - 1, 0), 1)
    before = lax.ppermute(
        jnp.broadcast_to(last_row, (8, D)), "dp", [(i, i + 1) for i in range(n - 1)]
    )
    gradient = table_pack(plan, place, grad_table, before)
    line = d * share + jnp.arange(share, dtype=jnp.int32)[:, None]
    flat_index = line * LANES + jnp.arange(LANES, dtype=jnp.int32)[None, :]
    gradient = jnp.where(flat_index < plan.table, gradient, 0.0)

    tail_grads = pack_tail(
        plan,
        [
            grad_attn_in,
            grad_attn_out,
            grad_ffn_in,
            grad_ffn_out,
            jnp.swapaxes(grad_shared, 0, 1),
            grad_qv,
            grad_up_bias,
        ],
    )
    if m == 2:
        other = lax.dynamic_index_in_dim(tail_grads, 1 - h, 0, keepdims=False)
        tail_grad = own_row(tail_grads) + swap(other, "head", 1, 2)
    else:
        tail_grad = lax.psum_scatter(tail_grads, "head", scatter_dimension=0, tiled=False)
    gradient = gradient + reduce_tail(plan, tail_grad)

    numbers = jnp.stack([jnp.sum(gradient * gradient), loss_local])
    numbers = total_all(jnp.zeros((8, LANES), F32).at[0, :2].set(numbers), plan)
    square_sum, loss_sum = numbers[0, 0], numbers[0, 1]
    grad_norm = jnp.sqrt(square_sum)
    clipped = gradient * (CLIP_NORM / jnp.maximum(grad_norm, CLIP_NORM))
    vector_start = plan.table + plan.width * D * 4 + 2 * D * plan.units + (LEN + 2) * plan.width
    matrix_part = flat_index < vector_start
    step_rate = jnp.where(matrix_part, RATE_MATRIX, RATE_VECTOR)
    decay_rate = jnp.where(matrix_part, WEIGHT_DECAY, 0.0)
    first_moment = first_moment.reshape(share, LANES)
    second_moment = second_moment.reshape(share, LANES)
    new_first = BETA_ONE * first_moment + (1.0 - BETA_ONE) * clipped
    new_second = BETA_TWO * second_moment + (1.0 - BETA_TWO) * clipped * clipped
    adam_step = (
        new_first
        / (1.0 - BETA_ONE**STEP)
        / (jnp.sqrt(new_second / (1.0 - BETA_TWO**STEP)) + ADAM_EPS)
    )
    new_master = chunk - step_rate * (adam_step + decay_rate * chunk)
    flat = lambda value: value.reshape(1, share_len)
    return (
        loss_sum,
        grad_norm,
        flat(new_master),
        flat(new_first),
        flat(new_second),
        flat(new_master.astype(BF16)),
    )


def solution(mesh):
    return jax.shard_map(
        local,
        mesh=mesh,
        in_specs=(
            P("head", "dp"),
            P("head", "dp"),
            P("head", "dp"),
            P("dp", None),
            P("dp", None),
            P("dp", None),
            P("dp", None),
            P("dp", None, None),
            P(None, None, "head"),
            P("dp", None, "head"),
        ),
        out_specs=(P(), P(), P("head", "dp"), P("head", "dp"), P("head", "dp"), P("head", "dp")),
        check_vma=False,
    )
```

time: 1730 us -> 587 us (0.34)
  waiting for transfers between devices: 820 us -> 144 us
  local copies, waits for them, and re-layouts: 524 us -> 117 us
  matrix products: 147 us -> 67.9 us
  starting transfers between devices: 13.8 us -> 91.7 us
  blocking collectives: 73.2 us -> 0 us
  Pallas kernels: 0 us -> 48.3 us
    unnamed x17 -> x0, waiting for transfers between devices: 576 us -> none
    slice x8 -> x14, local copies, waits for them, and re-layouts: 222 us -> 6.41 us  [the longest x1 1.25 us: local(): pick_tq = dot('hel,pl->hpe', teacher_proj[0], pick_hot).astype(BF16)]
    all_gather x1 -> x0, waiting for transfers between devices: 214 us -> none  [local(): lax.all_gather(master.astype(jnp.bfloat16), 'dp', axis=1, tiled=True)[0]]
    concatenate x3 -> x16, local copies, waits for them, and re-layouts: 165 us -> 6.91 us  [the longest x13 6.82 us: local(): jnp.concatenate([grad_positions, vectors]).reshape(SROWS, m, plan.width)]
    all_to_all x0 -> x9, waiting for transfers between devices: none -> 134 us  [the longest x1 45.5 us: local(): lax.all_to_all(blocks, 'dp', 0, 0, tiled=False).reshape(picks, plan.rows)]
    dot_general x44 -> x46, matrix products: 135 us -> 63 us  [dot(): return jnp.einsum(spec, left, right, preferred_element_type=F32, **options)]
    unnamed x300 -> x242, local copies, waits for them, and re-layouts: 12 us -> 74.9 us
    reshape x10 -> x2, local copies, waits for them, and re-layouts: 62.7 us -> 0.16 us  [the longest x1 0.09 us: local(): dot('hpl,hel->phe', prob_low, values).astype(BF16)]
  transfers between devices with their start and end apart: 15 -> 37, of which waited for: 6 -> 14; matrix products, arithmetic and copies ran while one was open for 12% -> 25% of each run, Pallas kernels for 0% -> 5%
where the time goes in v1:
time: 587 us; the launch traced here: 577 us
  waiting for transfers between devices  144 us (25%)
  local copies, waits for them, and re-layouts  117 us (20%)
  other arithmetic  97.6 us (17%)
  starting transfers between devices  91.7 us (16%)
  matrix products  67.9 us (12%)
  Pallas kernels  48.3 us (8%)
  between operations  9.48 us (2%)
    unnamed x242, local copies, waits for them, and re-layouts  74.9 us
    dot_general x46, matrix products, dot(): return jnp.einsum(spec, left, right, preferred_element_type=F32, **options)  63 us
    all_to_all x1, waiting for transfers between devices, local(): lax.all_to_all(blocks, 'dp', 0, 0, tiled=False).reshape(picks, plan.rows)  45.5 us
    all_to_all x3, waiting for transfers between devices, gather_to_all(): lax.all_to_all(jnp.broadcast_to(value[None], (plan.n,) + value.shape), 'd...  30.6 us
    all_to_all x1, waiting for transfers between devices, reduce_tail(): lax.all_to_all(both.reshape(n, size, LANES).astype(BF16), 'dp', 0, 0, til...  23.4 us
    pallas_call x1, Pallas kernels, map_attention(): pl.pallas_call(attention_kernel, out_shape=[jax.ShapeDtypeStruct((HEADS,...  22.5 us
    all_to_all x3, starting transfers between devices, gather_to_all(): lax.all_to_all(jnp.broadcast_to(value[None], (plan.n,) + value.shape), 'd...  21.9 us
    mul x1, other arithmetic, local(): new_second = BETA_TWO * second_moment + (1.0 - BETA_TWO) * clipped * clipped  16.8 us
  transfers between devices with their start and end apart: 37, of which 14 were waited for; matrix products, arithmetic and copies ran while one was open for 25% of the time, Pallas kernels for 5%

profile of v1, /device:TPU:0, one launch (start us, length us, event | category | flops | bytes accessed | tf_op | source)
XLA Modules:
  0.0 577.4 jit_solution(14021950312119443713)
XLA Ops:
  0.7 12.3 %reduce.8 = f32[338304]{0:T(1024)S(1)} reduce(f32[1,338304]{1,0:T(1,128)} %param.16, f32[]{:T(128)} %constant.394), dimensions={0}, to_apply=%param.16.reduce_sub_computation | reduce | bytes 2706436 | tf_op args[0]
  50.3 11.9 %all-to-all-start.4 = ((s32[32,1,128]{2,1,0:T(1,128)}), s32[32,1,128]{2,1,0:T(1,128)S(1)}, u32[]{:S(2)}, u32[]{:S(2)}) async-start(s32[32,1,128]{2,1,0:T(1,128)} %bitcast.16), calls=%async_computation.4 | async-start | bytes 32768 | tf_op jit(solution)/shard_map/all_to_all | solution.py:520
  64.6 4.8 all-to-all-done.4
  92.6 12.6 %all-to-all-done.6 = bf16[16,336,128]{2,1,0:T(8,128)(2,1)S(1)} async-done(((bf16[16,336,128]{2,1,0:T(8,128)(2,1)}), bf16[16,336,128]{2,1,0:T(8,128)(2,1)S(1)}, u32[]{:S(2)}, u32[]{:S(2)}) %all-to-all-start.6) | async-done | bytes 1376288 | tf_op jit(solution)/shard_map/all_to_all | solution.py:290
  105.4 6.4 %all-to-all-start.5 = ((bf16[32,32,312]{2,1,0:T(8,128)(2,1)}), bf16[32,32,312]{2,1,0:T(8,128)(2,1)}, u32[]{:S(2)}, u32[]{:S(2)}) async-start(bf16[32,32,312]{2,1,0:T(8,128)(2,1)} %bitcast.539), calls=%async_computation.5 | async-start | bytes 1572864 | tf_op jit(solution)/shard_map/all_to_all | solution.py:537
  117.4 14.9 %all-to-all-done.5 = bf16[32,32,312]{2,1,0:T(8,128)(2,1)} async-done(((bf16[32,32,312]{2,1,0:T(8,128)(2,1)}), bf16[32,32,312]{2,1,0:T(8,128)(2,1)}, u32[]{:S(2)}, u32[]{:S(2)}) %all-to-all-start.5) | async-done | bytes 639008 | tf_op jit(solution)/shard_map/all_to_all | solution.py:537
  138.8 7.5 %shard_map.146 = (bf16[2,936,156]{2,1,0:T(8,128)(2,1)}, bf16[2,156,312]{2,1,0:T(8,128)(2,1)}, bf16[2,312,600]{2,1,0:T(8,128)(2,1)}, bf16[2,600,312]{2,1,0:T(8,12...) custom-call(bf16[2,5136,128]{2,1,0:T(8,128)(2,1)} %pad_maximum_fusion.1.tail), custom_call_target="tpu_custom_call" | custom-call | tf_op jit(solution)/shard_map/pallas_call | solution.py:241
  166.5 4.7 all-to-all-start.7
  175.1 10.8 %all-to-all-done.7 = bf16[16,40,312]{2,1,0:T(8,128)(2,1)} async-done(((bf16[16,40,312]{2,1,0:T(8,128)(2,1)}), bf16[16,40,312]{2,1,0:T(8,128)(2,1)}, u32[]{:S(2)}, u32[]{:S(2)}) %all-to-all-start.7) | async-done | bytes 399392 | tf_op jit(solution)/shard_map/all_to_all | solution.py:290
  185.9 4.9 all-to-all-start.9
  190.9 4.7 copy.222
  202.0 45.5 %all-to-all-done.9 = bf16[16,80,1088]{2,1,0:T(8,128)(2,1)} async-done(((bf16[16,80,1088]{2,1,0:T(8,128)(2,1)}), bf16[16,80,1088]{2,1,0:T(8,128)(2,1)}, u32[]{:S(2)}, u32[]{:S(2)}) %all-to-all-start.9) | async-done | bytes 2785312 | tf_op jit(solution)/shard_map/all_to_all | solution.py:592
  247.5 4.7 bitcast_convert_fusion
  252.2 7.5 %copy.219 = f32[1280,1088]{0,1:T(8,128)} copy(f32[1280,1088]{1,0:T(8,128)} %bitcast_convert_fusion) | data formatting | bytes 11141120 | tf_op jit(solution)/shard_map/convert_element_type | solution.py:670
  262.3 6.4 %select_reduce_fusion.2 = (f32[]{:T(128)}, f32[1280]{0:T(1024)S(1)}) fusion(f32[1280,1088]{0,1:T(8,128)} %get-tuple-element.336, f32[1280,1088]{0,1:T(8,128)} %copy.219, f32[1280]{0:T(1024)S(1)} %fusion.89, pred[1088]{0:T(1024)(128)(4,1)S(1)} %iota_compare_fusion.50, f32[1280]{0:T(1024)S(1)} %get-tuple-element.335), kind=kLoop, calls=%fused_computation.34 | loop fusion | flops 12532479 | bytes 11157572 | tf_op jit(solution)/shard_map/reduce_sum | solution.py:677
  271.4 13.3 %all-to-all-start.8 = ((f32[16,2,1280]{2,1,0:T(2,128)}), f32[16,2,1280]{2,1,0:T(2,128)}, u32[]{:S(2)}, u32[]{:S(2)}) async-start(f32[16,2,1280]{2,1,0:T(2,128)} %broadcast_in_dim.381), calls=%async_computation.8 | async-start | bytes 327680 | tf_op jit(solution)/shard_map/all_to_all | solution.py:290
  286.1 7.2 %all-to-all-done.8 = f32[16,2,1280]{2,1,0:T(2,128)} async-done(((f32[16,2,1280]{2,1,0:T(2,128)}), f32[16,2,1280]{2,1,0:T(2,128)}, u32[]{:S(2)}, u32[]{:S(2)}) %all-to-all-start.8) | async-done | bytes 163872 | tf_op jit(solution)/shard_map/all_to_all | solution.py:290
  294.5 5.7 multiply_convert_fusion
  317.0 22.5 %shard_map.147 = (f32[12,32,512]{2,1,0:T(8,128)}, f32[12,32,512]{2,1,0:T(8,128)}, f32[1,512]{1,0:T(1,128)}) custom-call(bf16[3,12,32,512]{3,2,1,0:T(8,128)(2,1)} %bitcast.537, bf16[2,12,64,512]{3,2,1,0:T(8,128)(2,1)} %bitcast.535, s32[512,1]{1,0:T(8,128)} %copy.227.sent_col, s32[1,512]{1,0:T(1,128)} %bitcast.575, f32[512,1]{1,0:T(8,128)} %compare_convert_fusion.weight, ...), custom_call_target="tpu_custom_call" | custom-call | tf_op jit(solution)/shard_map/pallas_call | solution.py:403
  353.6 5.3 fusion.64
  358.9 5.5 fusion.65
  387.7 9.7 %shard_map.149 = f32[2,5136,128]{2,1,0:T(8,128)} custom-call(f32[2,936,156]{2,1,0:T(8,128)} %bitcast.534, f32[2,156,312]{2,1,0:T(8,128)} %fusion.66.refs_1_, f32[2,312,600]{2,1,0:T(8,128)} %convolution_bitcast_fusion.refs_2_, f32[2,600,312]{2,1,0:T(8,128)} %fusion.215.refs_3_, f32[2,522,156]{2,1,0:T(8,128)} %bitcast.538, ...), custom_call_target="tpu_custom_call" | custom-call | tf_op jit(solution)/shard_map/pallas_call | solution.py:271
  402.7 5.9 %all-to-all-start.11 = ((bf16[32,32,312]{2,1,0:T(8,128)(2,1)}), bf16[32,32,312]{2,1,0:T(8,128)(2,1)}, u32[]{:S(2)}, u32[]{:S(2)}) async-start(bf16[32,32,312]{2,1,0:T(8,128)(2,1)} %bitcast.113), calls=%async_computation.11 | async-start | bytes 1572864 | tf_op jit(solution)/shard_map/all_to_all | solution.py:755
  414.8 14.5 %all-to-all-done.11 = bf16[32,32,312]{2,1,0:T(8,128)(2,1)} async-done(((bf16[32,32,312]{2,1,0:T(8,128)(2,1)}), bf16[32,32,312]{2,1,0:T(8,128)(2,1)}, u32[]{:S(2)}, u32[]{:S(2)}) %all-to-all-start.11) | async-done | bytes 639008 | tf_op jit(solution)/shard_map/all_to_all | solution.py:755
  441.3 23.4 %all-to-all-done.12 = bf16[16,336,128]{2,1,0:T(8,128)(2,1)S(1)} async-done(((bf16[16,336,128]{2,1,0:T(8,128)(2,1)}), bf16[16,336,128]{2,1,0:T(8,128)(2,1)S(1)}, u32[]{:S(2)}, u32[]{:S(2)}) %all-to-all-start.12) | async-done | bytes 1376288 | tf_op jit(solution)/shard_map/all_to_all | solution.py:356
  464.8 7.6 %collective-permute-start.16 = (f32[336,128]{1,0:T(8,128)S(1)}, f32[336,128]{1,0:T(8,128)S(1)}, u32[]{:S(2)}, u32[]{:S(2)}) collective-permute-start(f32[336,128]{1,0:T(8,128)S(1)} %convert_reduce_fusion), channel_id=1, source_target_pairs={{0,28},{2,30},{1,29},{3,31}} | collective-permute-start | bytes 516104 | tf_op jit(solution)/shard_map/ppermute | solution.py:362
  509.6 6.4 %collective-permute-start.27 = (f32[8,128]{1,0:T(8,128)S(1)}, f32[8,128]{1,0:T(8,128)S(1)}, u32[]{:S(2)}, u32[]{:S(2)}) collective-permute-start(f32[8,128]{1,0:T(8,128)S(1)} %add.546), channel_id=1, source_target_pairs={{0,16},{2,18},{4,20},{6,22},{8,24},{10,26},{12,28},{14,30},{16,0},... | collective-permute-start | bytes 12296 | tf_op jit(solution)/shard_map/ppermute | solution.py:286
  516.1 16.8 %multiply_reduce_fusion.1 = (f32[338304]{0:T(1024)}, f32[338304]{0:T(1024)}) fusion(f32[1,338304]{1,0:T(1,128)} %param.18, f32[1,338304]{1,0:T(1,128)} %param.17), kind=kLoop, calls=%fused_computation.96 | loop fusion | flops 676608 | bytes 5412864 | tf_op jit(solution)/shard_map/mul | solution.py:810
  537.2 11.3 %copy.284 = bf16[1,1,2643,128]{3,1,2,0:T(2,128)(2,1)} copy(bf16[1,1,2643,128]{3,2,1,0:T(8,128)(2,1)S(1)} %get-tuple-element.265) | data formatting | bytes 1353216
  548.4 9.4 %copy.285 = f32[1,1,2643,128]{3,1,2,0:T(1,128)} copy(f32[1,1,2643,128]{3,2,1,0:T(8,128)S(1)} %get-tuple-element.282) | data formatting | bytes 2706432
  557.8 9.1 %copy.286 = f32[1,1,2643,128]{3,1,2,0:T(1,128)} copy(f32[1,1,2643,128]{3,2,1,0:T(8,128)S(1)} %get-tuple-element.283) | data formatting | bytes 2706432
  566.9 9.1 %copy.287 = f32[1,1,2643,128]{3,1,2,0:T(1,128)} copy(f32[1,1,2643,128]{3,2,1,0:T(8,128)S(1)} %bitcast.536) | data formatting | bytes 2706432
  (511 shorter events, 225.6 us)
Async XLA Ops:
  16.5 31.3 %collective-permute-start.1 = (bf16[336,128]{1,0:T(8,128)(2,1)}, bf16[336,128]{1,0:T(8,128)(2,1)S(1)}, u32[]{:S(2)}, u32[]{:S(2)}) collective-permute-start(bf16[336,128]{1,0:T(8,128)(2,1)} %get-tuple-element.303), channel_id=1, source_target_pairs={{28,24},{30,26},{29,25},{31,27}} | collective-permute-start | bytes 258056 | tf_op jit(solution)/shard_map/ppermute | solution.py:330
  17.1 31.4 %collective-permute-start.2 = (bf16[336,128]{1,0:T(8,128)(2,1)}, bf16[336,128]{1,0:T(8,128)(2,1)S(1)}, u32[]{:S(2)}, u32[]{:S(2)}) collective-permute-start(bf16[336,128]{1,0:T(8,128)(2,1)} %get-tuple-element.302), channel_id=1, source_target_pairs={{28,20},{30,22},{29,21},{31,23}} | collective-permute-start | bytes 258056 | tf_op jit(solution)/shard_map/ppermute | solution.py:330
  17.8 32.0 %collective-permute-start.3 = (bf16[336,128]{1,0:T(8,128)(2,1)}, bf16[336,128]{1,0:T(8,128)(2,1)S(1)}, u32[]{:S(2)}, u32[]{:S(2)}) collective-permute-start(bf16[336,128]{1,0:T(8,128)(2,1)} %get-tuple-element.301), channel_id=1, source_target_pairs={{28,16},{30,18},{29,17},{31,19}} | collective-permute-start | bytes 258056 | tf_op jit(solution)/shard_map/ppermute | solution.py:330
  18.5 43.7 %collective-permute-start.4 = (bf16[336,128]{1,0:T(8,128)(2,1)}, bf16[336,128]{1,0:T(8,128)(2,1)S(1)}, u32[]{:S(2)}, u32[]{:S(2)}) collective-permute-start(bf16[336,128]{1,0:T(8,128)(2,1)} %get-tuple-element.300), channel_id=1, source_target_pairs={{28,12},{30,14},{29,13},{31,15}} | collective-permute-start | bytes 258056 | tf_op jit(solution)/shard_map/ppermute | solution.py:330
  19.2 44.4 %collective-permute-start.5 = (bf16[336,128]{1,0:T(8,128)(2,1)S(1)}, bf16[336,128]{1,0:T(8,128)(2,1)S(1)}, u32[]{:S(2)}, u32[]{:S(2)}) collective-permute-start(bf16[336,128]{1,0:T(8,128)(2,1)S(1)} %get-tuple-element.299), channel_id=1, source_target_pairs={{28,8},{30,10},{29,9},{31,11}} | collective-permute-start | bytes 258056 | tf_op jit(solution)/shard_map/ppermute | solution.py:330
  47.8 15.7 %collective-permute-start.6 = (bf16[336,128]{1,0:T(8,128)(2,1)S(1)}, bf16[336,128]{1,0:T(8,128)(2,1)S(1)}, u32[]{:S(2)}, u32[]{:S(2)}) collective-permute-start(bf16[336,128]{1,0:T(8,128)(2,1)S(1)} %get-tuple-element.298), channel_id=1, source_target_pairs={{28,4},{30,6},{29,5},{31,7}} | collective-permute-start | bytes 258056 | tf_op jit(solution)/shard_map/ppermute | solution.py:330
  48.5 15.2 %collective-permute-start.7 = (bf16[336,128]{1,0:T(8,128)(2,1)S(1)}, bf16[336,128]{1,0:T(8,128)(2,1)S(1)}, u32[]{:S(2)}, u32[]{:S(2)}) collective-permute-start(bf16[336,128]{1,0:T(8,128)(2,1)S(1)} %get-tuple-element.297), channel_id=1, source_target_pairs={{28,0},{30,2},{29,1},{31,3}} | collective-permute-start | bytes 258056 | tf_op jit(solution)/shard_map/ppermute | solution.py:330
  49.8 66.3 %collective-permute-start.11 = (f32[2,80]{1,0:T(2,128)S(1)}, f32[2,80]{1,0:T(2,128)S(1)}, u32[]{:S(2)}, u32[]{:S(2)}) collective-permute-start(f32[2,80]{1,0:T(2,128)S(1)} %pad_maximum_fusion.13), channel_id=1, source_target_pairs={{0,1},{1,0},{2,3},{3,2},{4,5},{5,4},{6,7},{7,6},{8,9},{9,8},{10,11... | collective-permute-start | bytes 1928 | tf_op jit(solution)/shard_map/ppermute | solution.py:286
  50.3 19.0 %all-to-all-start.4 = ((s32[32,1,128]{2,1,0:T(1,128)}), s32[32,1,128]{2,1,0:T(1,128)S(1)}, u32[]{:S(2)}, u32[]{:S(2)}) async-start(s32[32,1,128]{2,1,0:T(1,128)} %bitcast.16), calls=%async_computation.4 | async-start | bytes 32768 | tf_op jit(solution)/shard_map/all_to_all | solution.py:520
  62.2 19.9 %collective-permute-start = (f32[8,128]{1,0:T(8,128)S(1)}, f32[8,128]{1,0:T(8,128)S(1)}, u32[]{:S(2)}, u32[]{:S(2)}) collective-permute-start(f32[8,128]{1,0:T(8,128)S(1)} %bitcast.588), channel_id=1, source_target_pairs={{2,0},{4,2},{6,4},{8,6},{10,8},{12,10},{14,12},{16,14},{18,16},{20... | collective-permute-start | bytes 12296 | tf_op jit(solution)/shard_map/ppermute | solution.py:528
  70.6 34.6 %all-to-all-start.6 = ((bf16[16,336,128]{2,1,0:T(8,128)(2,1)}), bf16[16,336,128]{2,1,0:T(8,128)(2,1)S(1)}, u32[]{:S(2)}, u32[]{:S(2)}) async-start(bf16[16,336,128]{2,1,0:T(8,128)(2,1)} %broadcast_in_dim.369), calls=%async_computation.6 | async-start | bytes 2752512 | tf_op jit(solution)/shard_map/all_to_all | solution.py:290
  105.4 27.0 %all-to-all-start.5 = ((bf16[32,32,312]{2,1,0:T(8,128)(2,1)}), bf16[32,32,312]{2,1,0:T(8,128)(2,1)}, u32[]{:S(2)}, u32[]{:S(2)}) async-start(bf16[32,32,312]{2,1,0:T(8,128)(2,1)} %bitcast.539), calls=%async_computation.5 | async-start | bytes 1572864 | tf_op jit(solution)/shard_map/all_to_all | solution.py:537
  113.1 22.0 %collective-permute-start.8 = (bf16[5136,128]{1,0:T(8,128)(2,1)}, bf16[5136,128]{1,0:T(8,128)(2,1)}, u32[]{:S(2)}, u32[]{:S(2)}) collective-permute-start(bf16[5136,128]{1,0:T(8,128)(2,1)} %fusion.60), channel_id=1, source_target_pairs={{0,1},{1,0},{2,3},{3,2},{4,5},{5,4},{6,7},{7,6},{8,9},{9,8},{10,11... | collective-permute-start | bytes 3944456 | tf_op jit(solution)/shard_map/ppermute | solution.py:286
  166.5 19.5 %all-to-all-start.7 = ((bf16[16,40,312]{2,1,0:T(8,128)(2,1)}), bf16[16,40,312]{2,1,0:T(8,128)(2,1)}, u32[]{:S(2)}, u32[]{:S(2)}) async-start(bf16[16,40,312]{2,1,0:T(8,128)(2,1)} %broadcast_in_dim.378), calls=%async_computation.7 | async-start | bytes 983040 | tf_op jit(solution)/shard_map/all_to_all | solution.py:290
  185.9 61.5 %all-to-all-start.9 = ((bf16[16,80,1088]{2,1,0:T(8,128)(2,1)}), bf16[16,80,1088]{2,1,0:T(8,128)(2,1)}, u32[]{:S(2)}, u32[]{:S(2)}) async-start(bf16[16,80,1088]{2,1,0:T(8,128)(2,1)} %pad_maximum_fusion), calls=%async_computation.9 | async-start | bytes 5898240 | tf_op jit(solution)/shard_map/all_to_all | solution.py:592
  190.8 5.4 collective-permute-start.9
  195.6 113.6 %collective-permute-start.12 = (bf16[768,2,384]{0,2,1:T(8,128)(2,1)}, bf16[768,2,384]{0,2,1:T(8,128)(2,1)}, u32[]{:S(2)}, u32[]{:S(2)}) collective-permute-start(bf16[768,2,384]{0,2,1:T(8,128)(2,1)} %copy.222), channel_id=1, source_target_pairs={{0,1},{1,0},{2,3},{3,2},{4,5},{5,4},{6,7},{7,6},{8,9},{9,8},{10,11... | collective-permute-start | bytes 3538952 | tf_op jit(solution)/shard_map/ppermute | solution.py:286
  271.4 21.9 %all-to-all-start.8 = ((f32[16,2,1280]{2,1,0:T(2,128)}), f32[16,2,1280]{2,1,0:T(2,128)}, u32[]{:S(2)}, u32[]{:S(2)}) async-start(f32[16,2,1280]{2,1,0:T(2,128)} %broadcast_in_dim.381), calls=%async_computation.8 | async-start | bytes 327680 | tf_op jit(solution)/shard_map/all_to_all | solution.py:290
  305.0 34.5 %all-to-all-start.10 = ((bf16[16,40,312]{2,1,0:T(8,128)(2,1)}), bf16[16,40,312]{2,1,0:T(8,128)(2,1)}, u32[]{:S(2)}, u32[]{:S(2)}) async-start(bf16[16,40,312]{2,1,0:T(8,128)(2,1)} %fusion.80), calls=%async_computation.10 | async-start | bytes 983040 | tf_op jit(solution)/shard_map/all_to_all | solution.py:689
  400.8 7.8 %collective-permute-start.15 = (f32[5136,128]{1,0:T(8,128)}, f32[5136,128]{1,0:T(8,128)}, u32[]{:S(2)}, u32[]{:S(2)}) collective-permute-start(f32[5136,128]{1,0:T(8,128)} %dynamic-slice_bitcast_fusion), channel_id=1, source_target_pairs={{0,1},{1,0},{2,3},{3,2},{4,5},{5,4},{6,7},{7,6},{8,9},{9,8},{10,11... | collective-permute-start | bytes 7888904 | tf_op jit(solution)/shard_map/ppermute | solution.py:286
  402.7 26.5 %all-to-all-start.11 = ((bf16[32,32,312]{2,1,0:T(8,128)(2,1)}), bf16[32,32,312]{2,1,0:T(8,128)(2,1)}, u32[]{:S(2)}, u32[]{:S(2)}) async-start(bf16[32,32,312]{2,1,0:T(8,128)(2,1)} %bitcast.113), calls=%async_computation.11 | async-start | bytes 1572864 | tf_op jit(solution)/shard_map/all_to_all | solution.py:755
  429.3 35.4 %all-to-all-start.12 = ((bf16[16,336,128]{2,1,0:T(8,128)(2,1)}), bf16[16,336,128]{2,1,0:T(8,128)(2,1)S(1)}, u32[]{:S(2)}, u32[]{:S(2)}) async-start(bf16[16,336,128]{2,1,0:T(8,128)(2,1)} %bitcast.132), calls=%async_computation.12 | async-start | bytes 2752512 | tf_op jit(solution)/shard_map/all_to_all | solution.py:356
  464.8 24.6 %collective-permute-start.16 = (f32[336,128]{1,0:T(8,128)S(1)}, f32[336,128]{1,0:T(8,128)S(1)}, u32[]{:S(2)}, u32[]{:S(2)}) collective-permute-start(f32[336,128]{1,0:T(8,128)S(1)} %convert_reduce_fusion), channel_id=1, source_target_pairs={{0,28},{2,30},{1,29},{3,31}} | collective-permute-start | bytes 516104 | tf_op jit(solution)/shard_map/ppermute | solution.py:362
  473.3 9.1 %collective-permute-start.14 = (f32[8,312]{1,0:T(8,128)S(1)}, f32[8,312]{1,0:T(8,128)S(1)}, u32[]{:S(2)}, u32[]{:S(2)}) collective-permute-start(f32[8,312]{1,0:T(8,128)S(1)} %broadcast_in_dim.393), channel_id=1, source_target_pairs={{0,2},{2,4},{4,6},{6,8},{8,10},{10,12},{12,14},{14,16},{16,18},{18... | collective-permute-start | bytes 29960 | tf_op jit(solution)/shard_map/ppermute | solution.py:771
  476.1 15.7 %collective-permute-start.17 = (f32[336,128]{1,0:T(8,128)S(1)}, f32[336,128]{1,0:T(8,128)S(1)}, u32[]{:S(2)}, u32[]{:S(2)}) collective-permute-start(f32[336,128]{1,0:T(8,128)S(1)} %convert_reduce_fusion), channel_id=1, source_target_pairs={{4,28},{6,30},{5,29},{7,31}} | collective-permute-start | bytes 516104 | tf_op jit(solution)/shard_map/ppermute | solution.py:362
  487.4 5.0 collective-permute-start.18
  488.1 4.4 collective-permute-start.19
  488.7 3.7 collective-permute-start.20
  498.7 3.7 collective-permute-start.24
  502.4 3.6 collective-permute-start.25
  506.0 3.6 collective-permute-start.26
  509.6 23.2 %collective-permute-start.27 = (f32[8,128]{1,0:T(8,128)S(1)}, f32[8,128]{1,0:T(8,128)S(1)}, u32[]{:S(2)}, u32[]{:S(2)}) collective-permute-start(f32[8,128]{1,0:T(8,128)S(1)} %add.546), channel_id=1, source_target_pairs={{0,16},{2,18},{4,20},{6,22},{8,24},{10,26},{12,28},{14,30},{16,0},... | collective-permute-start | bytes 12296 | tf_op jit(solution)/shard_map/ppermute | solution.py:286
  (111 other events, 1203.9 us)
